TPU v7x, 32 devices: a whole 2x2x4 slice. The times are simulated.
32 devices in a mesh: grp: 2 (over y), ex: 8 (over z, x), feat: 2 (over core).
Axes of the slice: x: 2, y: 2, z: 4, core: 2. Of those that a mesh axis runs over, the one named last changes fastest.
Arguments:
- slab_one: bfloat16 [4096, 4096], P(('grp', 'ex'), 'feat'), parts along dimension 0, may hold values from -6 to 6
- slab_two: bfloat16 [4096, 4096], P(('grp', 'ex'), 'feat'), parts along dimension 0, may hold values from -6 to 6
- target_product: bfloat16 [4096, 2048], P('feat', 'grp'), parts along dimension 1, may hold values from -0.09375 to 0.09375
Outputs:
- kernel_diag: float32 [2, 4096, 2048], P('feat', ('grp', 'ex')), parts along dimension 1
- kernel_cross: float32 [4096, 2048], P(('grp', 'ex', 'feat')), parts along dimension 0
- scores: bfloat16 [2, 4096, 1024], P(None, ('grp', 'ex'), 'feat'), parts along dimension 1
There are 2 independent parts, one for each index of `grp`. A program takes and returns all parts, laid end to end along the dimension named above; each array names one. Nothing has to cross between parts.
All inputs are finite; a program needn't handle non-finite values.
Results may differ from a plain program's by a relative error of at most 0.0004.
Values may be sent and summed in bfloat16 or wider, within the bound.
No kernel may reach another device: no remote copies, remote signals or barrier semaphores. Data moves between devices by JAX's collectives and lax.ppermute only.
A program may use at most 128 MiB of HBM per device.

v0:
```python
import math

import jax
import jax.numpy as jnp
from jax import lax
from jax.sharding import PartitionSpec as P


def gram_part(left, right):
    return lax.dot_general(
        left, right, (((0,), (0,)), ((), ())), preferred_element_type=jnp.float32
    )


def per_device(slab_one, slab_two, target_product):
    ex_devices = lax.axis_size("ex")
    feat_devices = lax.axis_size("feat")
    row_count, half_width = slab_one.shape
    factor = 1.0 / math.sqrt(row_count * ex_devices)
    feat_index = lax.axis_index("feat")
    cross_width = half_width // (ex_devices * feat_devices)
    gathered_one, gathered_two = (
        lax.all_gather(slab_one, "feat", axis=1, tiled=True),
        lax.all_gather(slab_two, "feat", axis=1, tiled=True),
    )
    total = jnp.zeros((half_width // ex_devices * lax.axis_size("ex"), half_width), jnp.float32)
    for slab_piece in (slab_one, slab_two):
        total = total + gram_part(slab_piece, slab_piece)
    diag_rows = lax.psum_scatter(total * factor, "ex", scatter_dimension=0, tiled=True)
    kernel_diag = diag_rows[None]

    def select_columns(gathered):
        first_half = gathered[:, :half_width].reshape(
            row_count, ex_devices, feat_devices, cross_width
        )
        chosen = lax.dynamic_index_in_dim(first_half, feat_index, 2, keepdims=False)
        return chosen.reshape(row_count, ex_devices * cross_width)

    operand_pairs = (
        (select_columns(gathered_one), gathered_one[:, half_width:]),
        (select_columns(gathered_two), gathered_two[:, half_width:]),
    )
    total = jnp.zeros((cross_width * lax.axis_size("ex"), half_width), jnp.float32)
    for left, right in operand_pairs:
        total = total + gram_part(left, right)
    kernel_cross = lax.psum_scatter(total * factor, "ex", scatter_dimension=0, tiled=True)
    target_half = lax.all_to_all(target_product, "feat", split_axis=1, concat_axis=0, tiled=True)
    scores = jnp.stack(
        [
            jnp.dot(gathered_one, target_half, preferred_element_type=jnp.float32),
            jnp.dot(gathered_two, target_half, preferred_element_type=jnp.float32),
        ]
    ).astype(jnp.bfloat16)
    return (kernel_diag, kernel_cross, scores)


def solution(mesh):
    in_specs = (P(("grp", "ex"), "feat"), P(("grp", "ex"), "feat"), P("feat", "grp"))
    out_specs = (
        P("feat", ("grp", "ex"), None),
        P(("grp", "ex", "feat"), None),
        P(None, ("grp", "ex"), "feat"),
    )
    return jax.shard_map(
        per_device, mesh=mesh, in_specs=in_specs, out_specs=out_specs, check_vma=False
    )
```

profile of v0, /device:TPU:0, one launch (start us, length us, event | category | flops | bytes accessed | tf_op | source)
XLA Modules:
  0.0 488.1 jit_solution(14393651511412813485)
XLA Ops:
  7.2 0.0 all-gather.3.cloned.1.call-start
  7.2 2.3 copy.6
  9.5 0.0 all-gather.3.cloned.1.call-update
  9.5 0.0 all-gather.5.cloned.1.call-start
  9.5 2.3 copy.7
  11.8 0.0 all-gather.5.cloned.1.call-update
  11.8 0.0 reduce-scatter.5.cloned.1.call-start
  11.9 11.5 %all-gather.3.cloned.1.call-done = bf16[256,4096]{0,1:T(8,128)(2,1)} async-done(((bf16[256,2048]{0,1:T(8,128)(2,1)}), bf16[256,4096]{0,1:T(8,128)(2,1)}) %all-gather.3.cloned.1.call-update) | async-done | bytes 2097168 | tf_op jit(solution)/shard_map/all_gather | solution.py:23
  23.4 0.0 copy-start.3
  23.4 1.4 slice.16
  24.9 12.4 %all-gather.5.cloned.1.call-done = bf16[256,4096]{0,1:T(8,128)(2,1)} async-done(((bf16[256,2048]{0,1:T(8,128)(2,1)}), bf16[256,4096]{0,1:T(8,128)(2,1)}) %all-gather.5.cloned.1.call-update) | async-done | bytes 2097168 | tf_op jit(solution)/shard_map/all_gather | solution.py:24
  37.3 1.3 slice.18
  38.7 0.0 copy-done.3
  38.7 0.0 copy-start.5
  38.7 1.3 fusion.3
  40.0 0.3 copy-done.5
  40.3 4.5 add_multiply_fusion.1
  44.8 0.0 copy-start.1
  44.8 0.0 reduce-scatter.5.cloned.1.call-update
  44.8 0.0 copy-start
  44.8 0.0 reduce-scatter.3.cloned.1.call-start
  44.9 1.1 copy-done.1
  46.0 2.4 fusion.5
  48.4 0.0 copy-done
  48.4 8.8 %add_multiply_fusion = f32[2048,2048]{1,0:T(8,128)} fusion(f32[2048,2048]{1,0:T(8,128)S(1)} %fusion.5, bf16[256,2048]{1,0:T(8,128)(2,1)S(1)} %copy-done), kind=kOutput, calls=%fused_computation | convolution fusion | flops 2155872256 | bytes 34603008 | tf_op jit(solution)/shard_map/dot_general | solution.py:10
  57.2 0.0 reduce-scatter.3.cloned.1.call-update
  57.2 6.6 %copy.8 = bf16[2048,1024]{0,1:T(8,128)(2,1)} copy(bf16[2048,1024]{1,0:T(8,128)(2,1)} %param.5) | data formatting | bytes 8388608 | tf_op args[2]
  63.7 11.8 %all_to_all.19 = bf16[2048,2,512]{0,2,1:T(8,128)(2,1)} all-to-all(bf16[2048,2,512]{0,2,1:T(8,128)(2,1)} %bitcast.23), channel_id=1, replica_groups=mesh['grp'=2,'ex'=8,'feat'=2] {'feat'}, dimensions={1} | all-to-all | bytes 8388608 | tf_op jit(solution)/shard_map/all_to_all | solution.py:47
  75.6 0.0 copy-start.6
  75.6 6.5 %copy.9 = bf16[2,2048,512]{2,1,0:T(8,128)(2,1)} copy(bf16[2,2048,512]{1,2,0:T(8,128)(2,1)} %bitcast.22) | data formatting | bytes 8388608 | tf_op jit(solution)/shard_map/all_to_all | solution.py:47
  82.0 0.0 copy-start.2
  82.0 0.0 copy-start.4
  82.0 0.0 copy-done.6
  82.0 3.8 fusion.1
  85.9 0.0 copy-done.2
  85.9 0.5 copy-done.4
  86.4 1.3 fusion
  87.7 0.8 pad_maximum_fusion
  88.5 106.7 %reduce-scatter.5.cloned.1.call-done = f32[128,2048]{1,0:T(8,128)} async-done(((f32[1024,2048]{1,0:T(8,128)}), f32[128,2048]{1,0:T(8,128)}) %reduce-scatter.5.cloned.1.call-update) | async-done | bytes 1048592 | tf_op jit(solution)/shard_map/reduce_scatter | solution.py:46
  195.2 286.4 %reduce-scatter.3.cloned.1.call-done = f32[256,2048]{1,0:T(8,128)} async-done(((f32[2048,2048]{1,0:T(8,128)}), f32[256,2048]{1,0:T(8,128)}) %reduce-scatter.3.cloned.1.call-update) | async-done | bytes 2097168 | tf_op jit(solution)/shard_map/reduce_scatter | solution.py:29
  (2 shorter events, 0.1 us)
Async XLA Ops:
  7.2 16.3 %all-gather.3.cloned.1.call-start = ((), (), s32[]{:S(2)}) async-start(), calls=%async_computation.4 | async-start | bytes 3145728 | tf_op jit(solution)/shard_map/all_gather | solution.py:23
  9.5 27.8 %all-gather.5.cloned.1.call-start = ((), (), s32[]{:S(2)}) async-start(), calls=%async_computation.5 | async-start | bytes 3145728 | tf_op jit(solution)/shard_map/all_gather | solution.py:24
  11.8 183.4 %reduce-scatter.5.cloned.1.call-start = ((), (), s32[]{:S(2)}) async-start(), calls=%async_computation.6 | async-start | bytes 9437184 | tf_op jit(solution)/shard_map/reduce_scatter | solution.py:46
  23.4 15.2 %copy-start.3 = (bf16[256,4096]{0,1:T(8,128)(2,1)S(1)}, bf16[256,4096]{0,1:T(8,128)(2,1)}, u32[]{:S(2)}) copy-start(bf16[256,4096]{0,1:T(8,128)(2,1)} %all-gather.3.cloned.1.call-done) | copy-start | bytes 6291460
  38.7 1.6 copy-start.5
  44.8 1.2 copy-start.1
  44.8 3.6 copy-start
  44.8 436.8 %reduce-scatter.3.cloned.1.call-start = ((), (), s32[]{:S(2)}) async-start(), calls=%async_computation.3 | async-start | bytes 18874368 | tf_op jit(solution)/shard_map/reduce_scatter | solution.py:29
  75.6 6.5 %copy-start.6 = (bf16[256,4096]{0,1:T(8,128)(2,1)S(1)}, bf16[256,4096]{0,1:T(8,128)(2,1)}, u32[]{:S(2)}) copy-start(bf16[256,4096]{0,1:T(8,128)(2,1)} %all-gather.5.cloned.1.call-done) | copy-start | bytes 6291460
  82.0 3.8 copy-start.2
  82.0 4.4 copy-start.4
Sparse Core Ops, SparseCore 0:
  10.1 13.2 all-gather.2
  25.5 11.7 all-gather.4
  44.9 150.2 reduce-scatter.4
  199.9 281.6 reduce-scatter.2
where the time goes:
time: 489 us; the launch traced here: 488 us
  waiting for transfers between devices  417 us (85%)
  local copies, waits for them, and re-layouts  22.3 us (5%)
  matrix products  22 us (4%)
  between operations  13.9 us (3%)
  blocking collectives  11.8 us (2%)
    reduce_scatter x2, waiting for transfers between devices, per_device(): lax.psum_scatter(total * factor, 'ex', scatter_dimension=0, tiled=True)  393 us
    dot_general x4, matrix products, gram_part(): lax.dot_general(left, right, (((0,), (0,)), ((), ())), preferred_element_...  16.9 us
    unnamed x17, local copies, waits for them, and re-layouts  13 us
    all_gather x1, waiting for transfers between devices, per_device(): lax.all_gather(slab_two, 'feat', axis=1, tiled=True)  12.4 us
    all_to_all x1, blocking collectives, per_device(): lax.all_to_all(target_product, 'feat', split_axis=1, concat_axis=0, tiled...  11.8 us
    all_gather x1, waiting for transfers between devices, per_device(): lax.all_gather(slab_one, 'feat', axis=1, tiled=True)  11.5 us
  transfers between devices with their start and end apart: 4, of which 4 were waited for; matrix products, arithmetic and copies ran while one was open for 7% of the time, Pallas kernels for 0%

commit v1 on v0

v1 whole, which is shorter than its diff:
```python
import math

import jax
import jax.numpy as jnp
from jax import lax
from jax.sharding import PartitionSpec as P


def gram_part(left, right):
    return lax.dot_general(
        left, right, (((0,), (0,)), ((), ())), preferred_element_type=jnp.float32
    )


def reducing(slab_one, slab_two, target_product):
    ex_devices = lax.axis_size("ex")
    feat_devices = lax.axis_size("feat")
    row_count, half_width = slab_one.shape
    factor = 1.0 / math.sqrt(row_count * ex_devices)
    feat_index = lax.axis_index("feat")
    cross_width = half_width // (ex_devices * feat_devices)
    gathered_one, gathered_two = (
        lax.all_gather(slab_one, "feat", axis=1, tiled=True),
        lax.all_gather(slab_two, "feat", axis=1, tiled=True),
    )
    total = gram_part(slab_one, slab_one) + gram_part(slab_two, slab_two)
    diag_rows = lax.psum_scatter(total * factor, "ex", scatter_dimension=0, tiled=True)
    kernel_diag = diag_rows[None]

    def select_columns(gathered):
        first_half = gathered[:, :half_width].reshape(
            row_count, ex_devices, feat_devices, cross_width
        )
        chosen = lax.dynamic_index_in_dim(first_half, feat_index, 2, keepdims=False)
        return chosen.reshape(row_count, ex_devices * cross_width)

    total = gram_part(select_columns(gathered_one), gathered_one[:, half_width:])
    total = total + gram_part(select_columns(gathered_two), gathered_two[:, half_width:])
    kernel_cross = lax.psum_scatter(total * factor, "ex", scatter_dimension=0, tiled=True)
    target_half = lax.all_to_all(target_product, "feat", split_axis=1, concat_axis=0, tiled=True)
    scores = jnp.stack(
        [
            jnp.dot(gathered_one, target_half, preferred_element_type=jnp.float32),
            jnp.dot(gathered_two, target_half, preferred_element_type=jnp.float32),
        ]
    ).astype(jnp.bfloat16)
    return (kernel_diag, kernel_cross, scores)


Z, X = 4, 2


def permute(value, moves):
    pairs = [
        ((fz * X + x) * 2 + fc, (tz * X + x) * 2 + tc)
        for (fz, fc), (tz, tc) in moves
        for x in range(X)
    ]
    return lax.ppermute(value, ("ex", "feat"), pairs)


def swap_x(value, holders):
    pairs = [
        ((z * X + x) * 2 + c, (z * X + 1 - x) * 2 + c) for z, c in holders for x in range(X)
    ]
    return lax.ppermute(value, ("ex", "feat"), pairs)


def swap_core(value):
    return lax.ppermute(value, "feat", [(0, 1), (1, 0)])


ENDS = ((0, 1), (3, 2))


def on_core(core, moves):
    return [((f, core), (t, core)) for f, t in moves]


IN = [(e, c) for e, c in ENDS]
OUT = [(c, e) for e, c in ENDS]
MID = [(1, 2), (2, 1)]
OVER = [(0, 2), (3, 1)]
HOLDERS = [(0, 1), (1, 0), (1, 1), (2, 0), (2, 1), (3, 1)]


def gathering(slab_one, slab_two, target_product):
    row_count, width = slab_one.shape
    factor = 1.0 / math.sqrt(row_count * Z * X)
    core = lax.axis_index("feat")
    ex = lax.axis_index("ex")
    z, x = ex // X, ex % X
    upper = z // 2
    centre = (z == 1) | (z == 2)
    group = width // Z
    half = width // 2
    block = width // (Z * X)

    def columns(half_index):
        return jnp.concatenate(
            [
                lax.dynamic_slice_in_dim(s, half_index * half, half, 1)
                for s in (slab_one, slab_two)
            ],
            0,
        )

    near, far = columns(upper), columns(1 - upper)

    a_moves = on_core(0, IN) + on_core(1, IN + OUT)
    b0n = permute(far, on_core(0, MID))
    c0n = permute(far, on_core(0, OVER))
    an = permute(near, a_moves)
    b1n = permute(far, on_core(1, MID))
    c1n = permute(far, on_core(1, OVER))
    af = permute(far, a_moves)
    b0f = permute(near, on_core(0, MID))
    c0f = permute(near, on_core(0, OVER))
    b1f = permute(near, on_core(1, MID))
    c1f = permute(near, on_core(1, OVER))

    targets = target_product.shape[1]
    half_targets = targets // 2

    def partial_scores(which):
        t = lax.dynamic_slice_in_dim(target_product, which * half_targets, half_targets, 1)
        return jnp.concatenate(
            [jnp.dot(s, t, preferred_element_type=jnp.float32) for s in (slab_one, slab_two)], 0
        )

    other_scores = swap_core(partial_scores(1 - core))
    scores = (partial_scores(core) + other_scores).astype(jnp.bfloat16)
    scores = scores.reshape(2, row_count, half_targets)

    mine = (z % 2) * group
    theirs = (1 - z % 2) * group

    def cut(value, start, size):
        return lax.dynamic_slice_in_dim(value, start, size, 1)

    given = permute(
        jnp.concatenate([cut(v, theirs, group) for v in (near, b0n, c0n)], 0),
        [((c, 0), (e, 1)) for e, c in ENDS],
    )
    across = lax.ppermute(
        jnp.concatenate([cut(v, mine, group) for v in (near, an, b0n, c0n)], 0),
        "feat",
        [(0, 1)],
    )
    rows = 2 * row_count
    first_block = jnp.concatenate(
        [across[:rows], jnp.where(centre, across[rows:], given)], 0
    )

    def arrived(core_zero, core_one, forwarded):
        return jnp.where(core == 0, core_zero, jnp.where(centre, core_one, forwarded))

    def gathered(own, a, b0, b1, c0, c1):
        db = permute(b1, on_core(1, OUT))
        dc = permute(c1, on_core(1, OUT))
        return jnp.concatenate([own, a, arrived(b0, b1, db), arrived(c0, c1, dc)], 0)

    all_near = gathered(near, an, b0n, b1n, c0n, c1n)

    def left(which):
        u = cut(all_near, mine + which * block, block)
        v = jnp.where(
            core == 0,
            cut(all_near, theirs + which * block, block),
            cut(first_block, which * block, block),
        )
        return jnp.concatenate([u, v], 1)

    left_other, left_mine = left(1 - x), left(x)

    def finish(right):
        other = swap_x(gram_part(left_other, right), HOLDERS)
        total = (gram_part(left_mine, right) + other) * factor
        end_diag = permute(total[block:], on_core(0, OUT))
        low_cross = lax.ppermute(total[block : block + block // 2], "feat", [(1, 0)])
        diag = jnp.where((core == 0) & ~centre, end_diag, total[:block])
        cross = jnp.where(core == 0, low_cross, total[block + block // 2 :])
        return diag, cross

    near_out = finish(all_near)
    all_far = gathered(far, af, b0f, b1f, c0f, c1f)
    far_out = finish(all_far)

    def assemble(n, f):
        return jnp.concatenate([jnp.where(upper == 0, n, f), jnp.where(upper == 0, f, n)], 1)

    kernel_diag = assemble(near_out[0], far_out[0])[None]
    kernel_cross = assemble(near_out[1], far_out[1])
    return (kernel_diag, kernel_cross, scores)


def solution(mesh):
    in_specs = (P(("grp", "ex"), "feat"), P(("grp", "ex"), "feat"), P("feat", "grp"))
    out_specs = (
        P("feat", ("grp", "ex"), None),
        P(("grp", "ex", "feat"), None),
        P(None, ("grp", "ex"), "feat"),
    )
    few = mesh.shape["ex"] == Z * X and mesh.shape["feat"] == 2
    return jax.shard_map(
        gathering if few else reducing,
        mesh=mesh,
        in_specs=in_specs,
        out_specs=out_specs,
        check_vma=False,
    )
```

time: 489 us -> 265 us (0.54)
  waiting for transfers between devices: 417 us -> 142 us
  starting transfers between devices: 0.16 us -> 62.2 us
  other arithmetic: 0.84 us -> 23.3 us
  between operations: 13.9 us -> 1.11 us
  blocking collectives: 11.8 us -> 0 us
  local copies, waits for them, and re-layouts: 22.3 us -> 11 us
    reduce_scatter x2 -> x0, waiting for transfers between devices: 393 us -> none  [per_device(): lax.psum_scatter(total * factor, 'ex', scatter_dimension=0, tiled=True)]
    ppermute x0 -> x23, waiting for transfers between devices: none -> 142 us  [the longest x17 119 us: permute(): return lax.ppermute(value, ('ex', 'feat'), pairs)]
    ppermute x0 -> x23, starting transfers between devices: none -> 62.2 us  [the longest x17 45.7 us: permute(): return lax.ppermute(value, ('ex', 'feat'), pairs)]
    all_gather x2 -> x0, waiting for transfers between devices: 23.9 us -> none  [the longest x1 12.4 us: per_device(): lax.all_gather(slab_two, 'feat', axis=1, tiled=True)]
    all_to_all x1 -> x0, blocking collectives: 11.8 us -> none  [per_device(): lax.all_to_all(target_product, 'feat', split_axis=1, concat_axis=0, tiled...]
    concatenate x0 -> x9, other arithmetic: none -> 11.4 us  [the longest x2 3.57 us: gathered(): jnp.concatenate([own, a, arrived(b0, b1, db), arrived(c0, c1, dc)], 0)]
    all_to_all x1 -> x0, local copies, waits for them, and re-layouts: 6.46 us -> none  [per_device(): lax.all_to_all(target_product, 'feat', split_axis=1, concat_axis=0, tiled...]
    unnamed x17 -> x28, local copies, waits for them, and re-layouts: 13 us -> 7.16 us
  transfers between devices with their start and end apart: 4 -> 23, of which waited for: 4 -> 8; matrix products, arithmetic and copies ran while one was open for 7% -> 17% of each run, Pallas kernels for 0% -> 0%
where the time goes in v1:
time: 265 us; the launch traced here: 264 us
  waiting for transfers between devices  142 us (54%)
  starting transfers between devices  62.2 us (23%)
  matrix products  24.5 us (9%)
  other arithmetic  23.3 us (9%)
  local copies, waits for them, and re-layouts  11 us (4%)
    ppermute x17, waiting for transfers between devices, permute(): return lax.ppermute(value, ('ex', 'feat'), pairs)  119 us
    ppermute x17, starting transfers between devices, permute(): return lax.ppermute(value, ('ex', 'feat'), pairs)  45.7 us
    ppermute x2, waiting for transfers between devices, finish(): low_cross = lax.ppermute(total[block:block + block // 2], 'feat', [(1, 0)])  22.6 us
    dot_general x4, matrix products, gram_part(): lax.dot_general(left, right, (((0,), (0,)), ((), ())), preferred_element_...  16.8 us
    dot_general x4, matrix products, partial_scores(): jnp.dot(s, t, preferred_element_type=jnp.float32)  7.7 us
    unnamed x28, local copies, waits for them, and re-layouts  7.16 us
    ppermute x1, starting transfers between devices, swap_core(): return lax.ppermute(value, 'feat', [(0, 1), (1, 0)])  7.01 us
  transfers between devices with their start and end apart: 23, of which 8 were waited for; matrix products, arithmetic and copies ran while one was open for 17% of the time, Pallas kernels for 0%

profile of v1, /device:TPU:0, one launch (start us, length us, event | category | flops | bytes accessed | tf_op | source)
XLA Modules:
  0.0 263.6 jit_solution(130734209401012282)
XLA Ops:
  0.7 2.5 constant_dynamic-update-slice_fusion.5
  3.2 1.3 constant_dynamic-update-slice_fusion.4
  4.5 1.0 pad_maximum_fusion.9
  5.5 5.0 %collective-permute-start.11 = (bf16[512,1024]{1,0:T(8,128)(2,1)}, bf16[512,1024]{1,0:T(8,128)(2,1)S(1)}, u32[]{:S(2)}, u32[]{:S(2)}) collective-permute-start(bf16[512,1024]{1,0:T(8,128)(2,1)} %pad_maximum_fusion.9), channel_id=1, source_target_pairs={{0,4},{2,6},{12,8},{14,10},{1,5},{3,7},{13,9},{15,11},{5,1},{7,3},... | collective-permute-start | bytes 3145736 | tf_op jit(solution)/shard_map/ppermute | solution.py:59
  10.5 0.7 collective-permute-start.1
  11.2 1.0 pad_maximum_fusion.8
  12.3 5.0 %collective-permute-start = (bf16[512,1024]{1,0:T(8,128)(2,1)}, bf16[512,1024]{1,0:T(8,128)(2,1)}, u32[]{:S(2)}, u32[]{:S(2)}) collective-permute-start(bf16[512,1024]{1,0:T(8,128)(2,1)} %pad_maximum_fusion.8), channel_id=1, source_target_pairs={{0,4},{2,6},{12,8},{14,10},{1,5},{3,7},{13,9},{15,11},{5,1},{7,3},... | collective-permute-start | bytes 3145736 | tf_op jit(solution)/shard_map/ppermute | solution.py:59
  17.2 1.3 collective-permute-start.4
  18.6 1.7 collective-permute-start.2
  20.3 14.0 %collective-permute-done.11 = bf16[512,1024]{1,0:T(8,128)(2,1)S(1)} collective-permute-done((bf16[512,1024]{1,0:T(8,128)(2,1)}, bf16[512,1024]{1,0:T(8,128)(2,1)S(1)}, u32[]{:S(2)}, u32[]{:S(2)}) %collective-permute-start.11) | collective-permute-done | bytes 1048608 | tf_op jit(solution)/shard_map/ppermute | solution.py:59
  34.3 1.7 collective-permute-start.5
  36.0 1.7 collective-permute-start.13
  37.6 19.1 %collective-permute-done = bf16[512,1024]{1,0:T(8,128)(2,1)} collective-permute-done((bf16[512,1024]{1,0:T(8,128)(2,1)}, bf16[512,1024]{1,0:T(8,128)(2,1)}, u32[]{:S(2)}, u32[]{:S(2)}) %collective-permute-start) | collective-permute-done | bytes 1048608 | tf_op jit(solution)/shard_map/ppermute | solution.py:59
  56.8 1.6 collective-permute-start.12
  58.4 0.9 fusion.27
  59.3 1.1 constant_dynamic-slice_fusion.5
  60.4 18.9 %collective-permute-done.4 = bf16[512,1024]{1,0:T(8,128)(2,1)S(1)} collective-permute-done((bf16[512,1024]{1,0:T(8,128)(2,1)}, bf16[512,1024]{1,0:T(8,128)(2,1)S(1)}, u32[]{:S(2)}, u32[]{:S(2)}) %collective-permute-start.4) | collective-permute-done | bytes 1048608 | tf_op jit(solution)/shard_map/ppermute | solution.py:59
  79.3 1.6 collective-permute-start.16
  80.9 0.1 constant_dynamic-slice_fusion.4
  81.0 1.7 collective-permute-start.3
  82.7 1.7 collective-permute-start.6
  84.4 0.9 constant_dynamic-slice_fusion.3
  85.3 1.5 pad_maximum_fusion
  86.7 2.6 %collective-permute-start.7 = (bf16[2048,512]{1,0:T(8,128)(2,1)}, bf16[2048,512]{1,0:T(8,128)(2,1)}, u32[]{:S(2)}, u32[]{:S(2)}) collective-permute-start(bf16[2048,512]{1,0:T(8,128)(2,1)} %pad_maximum_fusion), channel_id=1, source_target_pairs={{0,1},{2,3},{4,5},{6,7},{8,9},{10,11},{12,13},{14,15},{16,17},{18,... | collective-permute-start | bytes 6291464 | tf_op jit(solution)/shard_map/ppermute | solution.py:145
  89.4 0.7 collective-permute-start.14
  90.1 1.3 pad_maximum_fusion.3
  91.4 0.9 collective-permute-start.8
  92.3 2.3 constant_dynamic-update-slice_fusion
  94.6 17.2 %collective-permute-start.15 = (bf16[512,1024]{1,0:T(8,128)(2,1)}, bf16[512,1024]{1,0:T(8,128)(2,1)S(1)}, u32[]{:S(2)}, u32[]{:S(2)}) collective-permute-start(bf16[512,1024]{1,0:T(8,128)(2,1)} %pad_maximum_fusion.8), channel_id=1, source_target_pairs={{0,8},{2,10},{12,4},{14,6},{16,24},{18,26},{28,20},{30,22}} | collective-permute-start | bytes 3145736 | tf_op jit(solution)/shard_map/ppermute | solution.py:59
  111.8 0.7 collective-permute-start.17
  112.6 2.8 %select_dynamic-update-slice_fusion.3 = bf16[2048,1024]{1,0:T(8,128)(2,1)} fusion(bf16[2048,1024]{1,0:T(8,128)(2,1)} %constant_dynamic-update-slice_fusion, bf16[512,1024]{1,0:T(8,128)(2,1)S(1)} %collective-permute-done.1, bf16[512,1024]{1,0:T(8,128)(2,1)} %collective-permute-done.2, bf16[512,1024]{1,0:T(8,128)(2,1)} %collective-permute-done.3, pred[]{:T(512)S(6)} %or.3, ...), kind=kLoop, calls=%fused_computation.45 | loop fusion | flops 1048576 | bytes 4194306
  115.5 2.9 %select_dynamic-update-slice_fusion.2 = bf16[2048,1024]{1,0:T(8,128)(2,1)} fusion(bf16[2048,1024]{1,0:T(8,128)(2,1)} %select_dynamic-update-slice_fusion.3, bf16[512,1024]{1,0:T(8,128)(2,1)S(1)} %collective-permute-done.4, bf16[512,1024]{1,0:T(8,128)(2,1)} %collective-permute-done.5, bf16[512,1024]{1,0:T(8,128)(2,1)} %collective-permute-done.6, pred[]{:T(512)S(6)} %or.3, ...), kind=kLoop, calls=%fused_computation.44 | loop fusion | flops 1048576 | bytes 4194306 | tf_op jit(solution)/shard_map/concatenate | solution.py:161
  118.4 1.8 select_dynamic-update-slice_fusion.1
  120.3 4.1 %collective-permute-done.15 = bf16[512,1024]{1,0:T(8,128)(2,1)S(1)} collective-permute-done((bf16[512,1024]{1,0:T(8,128)(2,1)}, bf16[512,1024]{1,0:T(8,128)(2,1)S(1)}, u32[]{:S(2)}, u32[]{:S(2)}) %collective-permute-start.15) | collective-permute-done | bytes 1048608 | tf_op jit(solution)/shard_map/ppermute | solution.py:59
  124.4 0.6 select_dynamic-update-slice_fusion
  125.0 1.5 slice.40
  126.5 1.8 slice_select_fusion
  128.3 1.0 copy-done
  129.3 1.1 constant_dynamic-slice_fusion.6
  130.4 3.7 %fusion.8 = f32[512,1024]{1,0:T(8,128)} fusion(bf16[2048,1024]{1,0:T(8,128)(2,1)S(1)} %select_dynamic-update-slice_fusion, bf16[2048,256]{1,0:T(8,128)(2,1)S(1)} %get-tuple-element.19, bf16[2048,256]{1,0:T(8,128)(2,1)S(1)} %get-tuple-element.18), kind=kOutput, calls=%fused_computation.20 | convolution fusion | flops 2151677952 | bytes 8388608 | tf_op jit(solution)/shard_map/dot_general | solution.py:10
  134.0 2.2 collective-permute-start.18
  136.2 3.7 %fusion.9 = f32[512,1024]{1,0:T(8,128)} fusion(bf16[2048,1024]{1,0:T(8,128)(2,1)S(1)} %copy-done, bf16[2048,256]{1,0:T(8,128)(2,1)S(1)} %get-tuple-element.19, bf16[2048,256]{1,0:T(8,128)(2,1)S(1)} %get-tuple-element.18), kind=kOutput, calls=%fused_computation.21 | convolution fusion | flops 2151677952 | bytes 8388608 | tf_op jit(solution)/shard_map/dot_general | solution.py:10
  139.9 2.0 collective-permute-start.9
  141.9 2.4 fusion.16
  144.3 2.3 fusion.19
  146.6 1.0 pad_maximum_fusion.11
  147.6 7.0 %collective-permute-start.22 = (f32[512,512]{1,0:T(8,128)}, f32[512,512]{1,0:T(8,128)}, u32[]{:S(2)}, u32[]{:S(2)}) collective-permute-start(f32[512,512]{1,0:T(8,128)} %pad_maximum_fusion.11), channel_id=1, source_target_pairs={{0,1},{1,0},{2,3},{3,2},{4,5},{5,4},{6,7},{7,6},{8,9},{9,8},{10,11... | collective-permute-start | bytes 3145736 | tf_op jit(solution)/shard_map/ppermute | solution.py:70
  154.7 2.3 fusion.10
  157.0 5.3 %add_multiply_fusion = f32[512,1024]{1,0:T(8,128)S(1)} fusion(f32[512,1024]{1,0:T(8,128)} %collective-permute-done.18, bf16[2048,1024]{1,0:T(8,128)(2,1)} %copy-done.10, bf16[2048,256]{1,0:T(8,128)(2,1)S(1)} %get-tuple-element.20, bf16[2048,256]{1,0:T(8,128)(2,1)S(1)} %get-tuple-element.17), kind=kOutput, calls=%fused_computation.8 | convolution fusion | flops 2152726528 | bytes 10485760 | tf_op jit(solution)/shard_map/dot_general | solution.py:10
  162.5 4.1 %add_multiply_fusion.1 = f32[512,1024]{1,0:T(8,128)S(1)} fusion(f32[512,1024]{1,0:T(8,128)} %collective-permute-done.9, bf16[2048,1024]{1,0:T(8,128)(2,1)S(1)} %copy-done.1, bf16[2048,256]{1,0:T(8,128)(2,1)S(1)} %get-tuple-element.20, bf16[2048,256]{1,0:T(8,128)(2,1)S(1)} %get-tuple-element.17), kind=kOutput, calls=%fused_computation.9 | convolution fusion | flops 2152726528 | bytes 10485760 | tf_op jit(solution)/shard_map/dot_general | solution.py:10
  166.8 1.4 collective-permute-start.21
  168.2 1.3 collective-permute-start.20
  169.5 1.3 collective-permute-start.19
  170.8 1.3 collective-permute-start.10
  172.1 0.7 fusion.13
  172.9 2.2 fusion.26
  175.1 21.3 %collective-permute-done.21 = f32[128,1024]{1,0:T(8,128)S(1)} collective-permute-done((f32[128,1024]{1,0:T(8,128)S(1)}, f32[128,1024]{1,0:T(8,128)S(1)}, u32[]{:S(2)}, u32[]{:S(2)}) %collective-permute-start.21) | collective-permute-done | bytes 524320 | tf_op jit(solution)/shard_map/ppermute | solution.py:180
  196.4 1.3 collective-permute-done.20
  197.7 0.2 broadcast_select_fusion.3
  197.9 1.0 pad_maximum_fusion.10
  198.9 51.5 %collective-permute-done.19 = f32[256,1024]{1,0:T(8,128)S(1)} collective-permute-done((f32[256,1024]{1,0:T(8,128)S(1)}, f32[256,1024]{1,0:T(8,128)S(1)}, u32[]{:S(2)}, u32[]{:S(2)}) %collective-permute-start.19) | collective-permute-done | bytes 1048608 | tf_op jit(solution)/shard_map/ppermute | solution.py:59
  250.4 11.2 %collective-permute-done.10 = f32[256,1024]{1,0:T(8,128)S(1)} collective-permute-done((f32[256,1024]{1,0:T(8,128)S(1)}, f32[256,1024]{1,0:T(8,128)S(1)}, u32[]{:S(2)}, u32[]{:S(2)}) %collective-permute-start.10) | collective-permute-done | bytes 1048608 | tf_op jit(solution)/shard_map/ppermute | solution.py:59
  261.7 0.5 broadcast_select_fusion.1
  262.1 1.5 maximum_bitcast_fusion
  (43 shorter events, 0.4 us)
Async XLA Ops:
  0.6 2.6 copy-start.3
  5.5 28.8 %collective-permute-start.11 = (bf16[512,1024]{1,0:T(8,128)(2,1)}, bf16[512,1024]{1,0:T(8,128)(2,1)S(1)}, u32[]{:S(2)}, u32[]{:S(2)}) collective-permute-start(bf16[512,1024]{1,0:T(8,128)(2,1)} %pad_maximum_fusion.9), channel_id=1, source_target_pairs={{0,4},{2,6},{12,8},{14,10},{1,5},{3,7},{13,9},{15,11},{5,1},{7,3},... | collective-permute-start | bytes 3145736 | tf_op jit(solution)/shard_map/ppermute | solution.py:59
  10.5 25.5 %collective-permute-start.1 = (bf16[512,1024]{1,0:T(8,128)(2,1)}, bf16[512,1024]{1,0:T(8,128)(2,1)S(1)}, u32[]{:S(2)}, u32[]{:S(2)}) collective-permute-start(bf16[512,1024]{1,0:T(8,128)(2,1)} %pad_maximum_fusion.9), channel_id=1, source_target_pairs={{4,8},{6,10},{8,4},{10,6},{20,24},{22,26},{24,20},{26,22}} | collective-permute-start | bytes 3145736 | tf_op jit(solution)/shard_map/ppermute | solution.py:59
  12.3 44.5 %collective-permute-start = (bf16[512,1024]{1,0:T(8,128)(2,1)}, bf16[512,1024]{1,0:T(8,128)(2,1)}, u32[]{:S(2)}, u32[]{:S(2)}) collective-permute-start(bf16[512,1024]{1,0:T(8,128)(2,1)} %pad_maximum_fusion.8), channel_id=1, source_target_pairs={{0,4},{2,6},{12,8},{14,10},{1,5},{3,7},{13,9},{15,11},{5,1},{7,3},... | collective-permute-start | bytes 3145736 | tf_op jit(solution)/shard_map/ppermute | solution.py:59
  17.2 62.0 %collective-permute-start.4 = (bf16[512,1024]{1,0:T(8,128)(2,1)}, bf16[512,1024]{1,0:T(8,128)(2,1)S(1)}, u32[]{:S(2)}, u32[]{:S(2)}) collective-permute-start(bf16[512,1024]{1,0:T(8,128)(2,1)} %pad_maximum_fusion.9), channel_id=1, source_target_pairs={{0,8},{2,10},{12,4},{14,6},{16,24},{18,26},{28,20},{30,22}} | collective-permute-start | bytes 3145736 | tf_op jit(solution)/shard_map/ppermute | solution.py:59
  18.6 62.4 %collective-permute-start.2 = (bf16[512,1024]{1,0:T(8,128)(2,1)}, bf16[512,1024]{1,0:T(8,128)(2,1)}, u32[]{:S(2)}, u32[]{:S(2)}) collective-permute-start(bf16[512,1024]{1,0:T(8,128)(2,1)} %pad_maximum_fusion.9), channel_id=1, source_target_pairs={{5,9},{7,11},{9,5},{11,7},{21,25},{23,27},{25,21},{27,23}} | collective-permute-start | bytes 3145736 | tf_op jit(solution)/shard_map/ppermute | solution.py:59
  34.3 1.7 copy-start.7
  34.3 48.4 %collective-permute-start.5 = (bf16[512,1024]{1,0:T(8,128)(2,1)}, bf16[512,1024]{1,0:T(8,128)(2,1)}, u32[]{:S(2)}, u32[]{:S(2)}) collective-permute-start(bf16[512,1024]{1,0:T(8,128)(2,1)} %pad_maximum_fusion.9), channel_id=1, source_target_pairs={{1,9},{3,11},{13,5},{15,7},{17,25},{19,27},{29,21},{31,23}} | collective-permute-start | bytes 3145736 | tf_op jit(solution)/shard_map/ppermute | solution.py:59
  36.0 50.8 %collective-permute-start.13 = (bf16[512,1024]{1,0:T(8,128)(2,1)}, bf16[512,1024]{1,0:T(8,128)(2,1)}, u32[]{:S(2)}, u32[]{:S(2)}) collective-permute-start(bf16[512,1024]{1,0:T(8,128)(2,1)} %pad_maximum_fusion.8), channel_id=1, source_target_pairs={{5,9},{7,11},{9,5},{11,7},{21,25},{23,27},{25,21},{27,23}} | collective-permute-start | bytes 3145736 | tf_op jit(solution)/shard_map/ppermute | solution.py:59
  56.8 32.6 %collective-permute-start.12 = (bf16[512,1024]{1,0:T(8,128)(2,1)}, bf16[512,1024]{1,0:T(8,128)(2,1)}, u32[]{:S(2)}, u32[]{:S(2)}) collective-permute-start(bf16[512,1024]{1,0:T(8,128)(2,1)} %pad_maximum_fusion.8), channel_id=1, source_target_pairs={{4,8},{6,10},{8,4},{10,6},{20,24},{22,26},{24,20},{26,22}} | collective-permute-start | bytes 3145736 | tf_op jit(solution)/shard_map/ppermute | solution.py:59
  79.3 12.1 %collective-permute-start.16 = (bf16[512,1024]{1,0:T(8,128)(2,1)}, bf16[512,1024]{1,0:T(8,128)(2,1)}, u32[]{:S(2)}, u32[]{:S(2)}) collective-permute-start(bf16[512,1024]{1,0:T(8,128)(2,1)} %pad_maximum_fusion.8), channel_id=1, source_target_pairs={{1,9},{3,11},{13,5},{15,7},{17,25},{19,27},{29,21},{31,23}} | collective-permute-start | bytes 3145736 | tf_op jit(solution)/shard_map/ppermute | solution.py:59
  81.0 13.6 %collective-permute-start.3 = (bf16[512,1024]{1,0:T(8,128)(2,1)}, bf16[512,1024]{1,0:T(8,128)(2,1)}, u32[]{:S(2)}, u32[]{:S(2)}) collective-permute-start(bf16[512,1024]{1,0:T(8,128)(2,1)} %collective-permute-done.2), channel_id=1, source_target_pairs={{5,1},{7,3},{9,13},{11,15},{21,17},{23,19},{25,29},{27,31}} | collective-permute-start | bytes 3145736 | tf_op jit(solution)/shard_map/ppermute | solution.py:59
  82.7 29.1 %collective-permute-start.6 = (bf16[512,1024]{1,0:T(8,128)(2,1)}, bf16[512,1024]{1,0:T(8,128)(2,1)}, u32[]{:S(2)}, u32[]{:S(2)}) collective-permute-start(bf16[512,1024]{1,0:T(8,128)(2,1)} %collective-permute-done.5), channel_id=1, source_target_pairs={{5,1},{7,3},{9,13},{11,15},{21,17},{23,19},{25,29},{27,31}} | collective-permute-start | bytes 3145736 | tf_op jit(solution)/shard_map/ppermute | solution.py:59
  85.3 4.8 %copy-start.2 = (bf16[512,512]{1,0:T(8,128)(2,1)S(1)}, bf16[512,512]{1,0:T(8,128)(2,1)}, u32[]{:S(2)}) copy-start(bf16[512,512]{1,0:T(8,128)(2,1)} %get-tuple-element.22) | copy-start | bytes 1572868
  86.7 38.3 %collective-permute-start.7 = (bf16[2048,512]{1,0:T(8,128)(2,1)}, bf16[2048,512]{1,0:T(8,128)(2,1)}, u32[]{:S(2)}, u32[]{:S(2)}) collective-permute-start(bf16[2048,512]{1,0:T(8,128)(2,1)} %pad_maximum_fusion), channel_id=1, source_target_pairs={{0,1},{2,3},{4,5},{6,7},{8,9},{10,11},{12,13},{14,15},{16,17},{18,... | collective-permute-start | bytes 6291464 | tf_op jit(solution)/shard_map/ppermute | solution.py:145
  89.4 29.1 %collective-permute-start.14 = (bf16[512,1024]{1,0:T(8,128)(2,1)}, bf16[512,1024]{1,0:T(8,128)(2,1)S(1)}, u32[]{:S(2)}, u32[]{:S(2)}) collective-permute-start(bf16[512,1024]{1,0:T(8,128)(2,1)} %collective-permute-done.13), channel_id=1, source_target_pairs={{5,1},{7,3},{9,13},{11,15},{21,17},{23,19},{25,29},{27,31}} | collective-permute-start | bytes 3145736 | tf_op jit(solution)/shard_map/ppermute | solution.py:59
  90.1 22.5 %copy-start.8 = (bf16[512,1024]{1,0:T(8,128)(2,1)S(1)}, bf16[512,1024]{1,0:T(8,128)(2,1)}, u32[]{:S(2)}) copy-start(bf16[512,1024]{1,0:T(8,128)(2,1)} %copy-done.7) | copy-start | bytes 3145732
  90.1 22.5 %copy-start.9 = (bf16[2048,1024]{1,0:T(8,128)(2,1)S(1)}, bf16[2048,1024]{1,0:T(8,128)(2,1)}, u32[]{:S(2)}) copy-start(bf16[2048,1024]{1,0:T(8,128)(2,1)} %get-tuple-element.3) | copy-start | bytes 12582916
  91.4 35.1 %collective-permute-start.8 = (bf16[1536,512]{1,0:T(8,128)(2,1)S(1)}, bf16[1536,512]{1,0:T(8,128)(2,1)S(1)}, u32[]{:S(2)}, u32[]{:S(2)}) collective-permute-start(bf16[1536,512]{1,0:T(8,128)(2,1)S(1)} %pad_maximum_fusion.3), channel_id=1, source_target_pairs={{4,1},{6,3},{8,13},{10,15},{20,17},{22,19},{24,29},{26,31}} | collective-permute-start | bytes 4718600 | tf_op jit(solution)/shard_map/ppermute | solution.py:59
  94.6 29.7 %collective-permute-start.15 = (bf16[512,1024]{1,0:T(8,128)(2,1)}, bf16[512,1024]{1,0:T(8,128)(2,1)S(1)}, u32[]{:S(2)}, u32[]{:S(2)}) collective-permute-start(bf16[512,1024]{1,0:T(8,128)(2,1)} %pad_maximum_fusion.8), channel_id=1, source_target_pairs={{0,8},{2,10},{12,4},{14,6},{16,24},{18,26},{28,20},{30,22}} | collective-permute-start | bytes 3145736 | tf_op jit(solution)/shard_map/ppermute | solution.py:59
  111.8 12.5 %collective-permute-start.17 = (bf16[512,1024]{1,0:T(8,128)(2,1)}, bf16[512,1024]{1,0:T(8,128)(2,1)S(1)}, u32[]{:S(2)}, u32[]{:S(2)}) collective-permute-start(bf16[512,1024]{1,0:T(8,128)(2,1)} %collective-permute-done.16), channel_id=1, source_target_pairs={{5,1},{7,3},{9,13},{11,15},{21,17},{23,19},{25,29},{27,31}} | collective-permute-start | bytes 3145736 | tf_op jit(solution)/shard_map/ppermute | solution.py:59
  125.0 5.4 %copy-start.10 = (bf16[2048,1024]{1,0:T(8,128)(2,1)}, bf16[2048,1024]{1,0:T(8,128)(2,1)S(1)}, u32[]{:S(2)}) copy-start(bf16[2048,1024]{1,0:T(8,128)(2,1)S(1)} %select_dynamic-update-slice_fusion) | copy-start | bytes 12582916
  126.5 2.8 %copy-start = (bf16[2048,1024]{1,0:T(8,128)(2,1)S(1)}, bf16[2048,1024]{1,0:T(8,128)(2,1)}, u32[]{:S(2)}) copy-start(bf16[2048,1024]{1,0:T(8,128)(2,1)} %select_dynamic-update-slice_fusion.2) | copy-start | bytes 12582916
  134.0 7.9 %copy-start.4 = (bf16[256,2048]{1,0:T(8,128)(2,1)S(1)}, bf16[256,2048]{1,0:T(8,128)(2,1)}, u32[]{:S(2)}) copy-start(bf16[256,2048]{1,0:T(8,128)(2,1)} %param.4) | copy-start | bytes 3145732
  134.0 22.9 %collective-permute-start.18 = (f32[512,1024]{1,0:T(8,128)}, f32[512,1024]{1,0:T(8,128)}, u32[]{:S(2)}, u32[]{:S(2)}) collective-permute-start(f32[512,1024]{1,0:T(8,128)} %fusion.8), channel_id=1, source_target_pairs={{1,3},{3,1},{4,6},{6,4},{5,7},{7,5},{8,10},{10,8},{9,11},{11,9},{1... | collective-permute-start | bytes 6291464 | tf_op jit(solution)/shard_map/ppermute | solution.py:66
  139.9 22.6 %collective-permute-start.9 = (f32[512,1024]{1,0:T(8,128)}, f32[512,1024]{1,0:T(8,128)}, u32[]{:S(2)}, u32[]{:S(2)}) collective-permute-start(f32[512,1024]{1,0:T(8,128)} %fusion.9), channel_id=1, source_target_pairs={{1,3},{3,1},{4,6},{6,4},{5,7},{7,5},{8,10},{10,8},{9,11},{11,9},{1... | collective-permute-start | bytes 6291464 | tf_op jit(solution)/shard_map/ppermute | solution.py:66
  141.9 2.4 copy-start.5
  147.6 25.2 %collective-permute-start.22 = (f32[512,512]{1,0:T(8,128)}, f32[512,512]{1,0:T(8,128)}, u32[]{:S(2)}, u32[]{:S(2)}) collective-permute-start(f32[512,512]{1,0:T(8,128)} %pad_maximum_fusion.11), channel_id=1, source_target_pairs={{0,1},{1,0},{2,3},{3,2},{4,5},{5,4},{6,7},{7,6},{8,9},{9,8},{10,11... | collective-permute-start | bytes 3145736 | tf_op jit(solution)/shard_map/ppermute | solution.py:70
  157.0 5.5 %copy-start.1 = (bf16[2048,1024]{1,0:T(8,128)(2,1)S(1)}, bf16[2048,1024]{1,0:T(8,128)(2,1)}, u32[]{:S(2)}) copy-start(bf16[2048,1024]{1,0:T(8,128)(2,1)} %select_dynamic-update-slice_fusion.2) | copy-start | bytes 12582916
  162.5 9.6 %copy-start.11 = (bf16[2048,1024]{1,0:T(8,128)(2,1)S(1)}, bf16[2048,1024]{1,0:T(8,128)(2,1)}, u32[]{:S(2)}) copy-start(bf16[2048,1024]{1,0:T(8,128)(2,1)} %param.5) | copy-start | bytes 12582916
  166.6 5.5 %copy-start.6 = (bf16[256,2048]{1,0:T(8,128)(2,1)S(1)}, bf16[256,2048]{1,0:T(8,128)(2,1)}, u32[]{:S(2)}) copy-start(bf16[256,2048]{1,0:T(8,128)(2,1)} %param.3) | copy-start | bytes 3145732
  166.8 29.6 %collective-permute-start.21 = (f32[128,1024]{1,0:T(8,128)S(1)}, f32[128,1024]{1,0:T(8,128)S(1)}, u32[]{:S(2)}, u32[]{:S(2)}) collective-permute-start(f32[128,1024]{1,0:T(8,128)S(1)} %slice.48), channel_id=1, source_target_pairs={{1,0},{3,2},{5,4},{7,6},{9,8},{11,10},{13,12},{15,14},{17,16},{19,... | collective-permute-start | bytes 1572872 | tf_op jit(solution)/shard_map/ppermute | solution.py:180
  168.2 29.5 %collective-permute-start.20 = (f32[128,1024]{1,0:T(8,128)S(1)}, f32[128,1024]{1,0:T(8,128)S(1)}, u32[]{:S(2)}, u32[]{:S(2)}) collective-permute-start(f32[128,1024]{1,0:T(8,128)S(1)} %slice.46), channel_id=1, source_target_pairs={{1,0},{3,2},{5,4},{7,6},{9,8},{11,10},{13,12},{15,14},{17,16},{19,... | collective-permute-start | bytes 1572872 | tf_op jit(solution)/shard_map/ppermute | solution.py:180
  169.5 80.9 %collective-permute-start.19 = (f32[256,1024]{1,0:T(8,128)S(1)}, f32[256,1024]{1,0:T(8,128)S(1)}, u32[]{:S(2)}, u32[]{:S(2)}) collective-permute-start(f32[256,1024]{1,0:T(8,128)S(1)} %slice.44), channel_id=1, source_target_pairs={{4,0},{6,2},{8,12},{10,14},{20,16},{22,18},{24,28},{26,30}} | collective-permute-start | bytes 3145736 | tf_op jit(solution)/shard_map/ppermute | solution.py:59
  170.8 90.9 %collective-permute-start.10 = (f32[256,1024]{1,0:T(8,128)S(1)}, f32[256,1024]{1,0:T(8,128)S(1)}, u32[]{:S(2)}, u32[]{:S(2)}) collective-permute-start(f32[256,1024]{1,0:T(8,128)S(1)} %slice.42), channel_id=1, source_target_pairs={{4,0},{6,2},{8,12},{10,14},{20,16},{22,18},{24,28},{26,30}} | collective-permute-start | bytes 3145736 | tf_op jit(solution)/shard_map/ppermute | solution.py:59

commit v2 on v0

v2 whole, which is shorter than its diff:
```python
import math

import jax
import jax.numpy as jnp
from jax import lax
from jax.sharding import PartitionSpec as P


def gram_part(left, right):
    return lax.dot_general(
        left, right, (((0,), (0,)), ((), ())), preferred_element_type=jnp.float32
    )


def reducing(slab_one, slab_two, target_product):
    ex_devices = lax.axis_size("ex")
    feat_devices = lax.axis_size("feat")
    row_count, half_width = slab_one.shape
    factor = 1.0 / math.sqrt(row_count * ex_devices)
    feat_index = lax.axis_index("feat")
    cross_width = half_width // (ex_devices * feat_devices)
    gathered_one, gathered_two = (
        lax.all_gather(slab_one, "feat", axis=1, tiled=True),
        lax.all_gather(slab_two, "feat", axis=1, tiled=True),
    )
    total = gram_part(slab_one, slab_one) + gram_part(slab_two, slab_two)
    diag_rows = lax.psum_scatter(total * factor, "ex", scatter_dimension=0, tiled=True)
    kernel_diag = diag_rows[None]

    def select_columns(gathered):
        first_half = gathered[:, :half_width].reshape(
            row_count, ex_devices, feat_devices, cross_width
        )
        chosen = lax.dynamic_index_in_dim(first_half, feat_index, 2, keepdims=False)
        return chosen.reshape(row_count, ex_devices * cross_width)

    total = gram_part(select_columns(gathered_one), gathered_one[:, half_width:])
    total = total + gram_part(select_columns(gathered_two), gathered_two[:, half_width:])
    kernel_cross = lax.psum_scatter(total * factor, "ex", scatter_dimension=0, tiled=True)
    target_half = lax.all_to_all(target_product, "feat", split_axis=1, concat_axis=0, tiled=True)
    scores = jnp.stack(
        [
            jnp.dot(gathered_one, target_half, preferred_element_type=jnp.float32),
            jnp.dot(gathered_two, target_half, preferred_element_type=jnp.float32),
        ]
    ).astype(jnp.bfloat16)
    return (kernel_diag, kernel_cross, scores)


Z, X = 4, 2


def permute(value, moves):
    pairs = [
        ((fz * X + x) * 2 + fc, (tz * X + x) * 2 + tc)
        for (fz, fc), (tz, tc) in moves
        for x in range(X)
    ]
    return lax.ppermute(value, ("ex", "feat"), pairs)


def swap_x(value, holders):
    pairs = [
        ((z * X + x) * 2 + c, (z * X + 1 - x) * 2 + c) for z, c in holders for x in range(X)
    ]
    return lax.ppermute(value, ("ex", "feat"), pairs)


def swap_core(value):
    return lax.ppermute(value, "feat", [(0, 1), (1, 0)])


ENDS = ((0, 1), (3, 2))


def on_core(core, moves):
    return [((f, core), (t, core)) for f, t in moves]


IN = [(e, c) for e, c in ENDS]
OUT = [(c, e) for e, c in ENDS]
MID = [(1, 2), (2, 1)]
OVER = [(0, 2), (3, 1)]
BOTH = lambda moves: on_core(0, moves) + on_core(1, moves)
CENTRES = [(1, 0), (1, 1), (2, 0), (2, 1)]
CENTRES_ONE = [(1, 1), (2, 1)]
ENDS_ONE = [(0, 1), (3, 1)]


def after(value, *earlier):
    return lax.optimization_barrier((value, *earlier))[0]


def gathering(slab_one, slab_two, target_product):
    row_count, width = slab_one.shape
    rows = 2 * row_count
    factor = 1.0 / math.sqrt(row_count * Z * X)
    core = lax.axis_index("feat")
    ex = lax.axis_index("ex")
    z, x = ex // X, ex % X
    lower = z < 2
    centre = (z == 1) | (z == 2)
    group = width // Z
    block = width // (Z * X)

    def own(below):
        start = jnp.where(lower, below, 3 - below) * group
        return jnp.concatenate(
            [lax.dynamic_slice_in_dim(s, start, group, 1) for s in (slab_one, slab_two)], 0
        )

    mine = [own(1), own(0), own(2), own(3)]
    sent = [mine[2], mine[3], mine[0], mine[1]]

    a_moves = on_core(0, IN) + on_core(1, IN + OUT)
    wide = [jnp.concatenate(mine[i : i + 2], 1) for i in (0, 2)]
    a, b, c = [None] * 4, [None] * 4, [None] * 4

    def gather(k, for_b=(), for_c=(), for_a=()):
        sb, sc = sent[k], sent[k]
        if k >= 1:
            sb, sc = after(sb, b[k - 1], *for_b), after(sc, c[k - 1], *for_c)
        with jax.named_scope(f"middle{k}"):
            b[k] = permute(sb, BOTH(MID))
        with jax.named_scope(f"over{k}"):
            c[k] = permute(sc, BOTH(OVER))
        if k % 2 == 0:
            with jax.named_scope(f"half{k}"):
                moved = permute(after(wide[k // 2], *for_a) if k else wide[0], a_moves)
            a[k], a[k + 1] = moved[:, :group], moved[:, group:]

    def put(k):
        return jnp.concatenate([a[k], mine[k], b[k], c[k]], 0)

    def forward(k, *earlier):
        with jax.named_scope(f"forward{k}"):
            return permute(after(at_centre[k][rows * 2 :], *earlier), on_core(1, OUT))

    def cut(value, which):
        return lax.dynamic_slice_in_dim(value, which * block, block, 1)

    def lefts(u, v):
        return [jnp.concatenate([cut(u, w), cut(v, w)], 1) for w in (1 - x, x)]

    def part(name, left_other, right):
        with jax.named_scope(name):
            return gram_part(left_other, right)

    def swap(name, value, holders):
        with jax.named_scope(name):
            return swap_x(value, holders)

    def total(name, left_mine, right, other):
        with jax.named_scope(name):
            return (gram_part(left_mine, right) + other) * factor

    at_centre, d = [None] * 4, [None] * 4
    gather(0)
    at_centre[0] = put(0)
    pu0 = part("cu0", cut(at_centre[0], 1 - x), at_centre[0])
    gather(1, (), (pu0,))
    xu0 = swap("cu0", pu0, CENTRES)
    with jax.named_scope("across"):
        across = lax.ppermute(
            jnp.concatenate(
                [jnp.where(centre, at_centre[0][:rows], mine[1]), at_centre[0][rows:]], 0
            ),
            "feat",
            [(0, 1)],
        )
    d[0] = forward(0)
    at_centre[1] = put(1)
    centre_v = jnp.where(core == 0, at_centre[1], across)
    cl = lefts(at_centre[0], centre_v)
    p1 = part("c1", cl[0], at_centre[1])
    pv0 = part("cv0", cut(centre_v, 1 - x), at_centre[0])
    gather(2, (xu0,), (p1, pv0), (d[0],))
    x1 = swap("c1", after(p1, xu0), CENTRES)
    xv0 = swap("cv0", pv0, CENTRES)
    d[1] = forward(1, d[0])
    with jax.named_scope("given"):
        given = permute(after(at_centre[1][rows:], d[0]), [((cz, 0), (ez, 1)) for ez, cz in ENDS])
    at_centre[2] = put(2)
    p2 = part("c2", cl[0], at_centre[2])

    def at_end(k):
        return jnp.concatenate([mine[k], a[k], d[k]], 0)

    end_own = at_end(1)
    end_given = jnp.concatenate([across[:rows], given], 0)
    el = lefts(end_own, end_given)
    near = jnp.concatenate([at_end(0), end_own], 1)
    pe0 = part("e0", el[0], near)
    gather(3, (xv0,), (p2, d[1]))
    xe0 = swap("e0", pe0, ENDS_ONE)

    x2 = swap("c2", after(p2, x1, xv0), CENTRES)
    d[2] = forward(2, d[1])
    at_centre[3] = put(3)
    p3 = part("c3", cl[0], after(at_centre[3], x1, pe0))
    pe2 = part("e2", el[0], at_end(2))
    xe2 = swap("e2", after(pe2, xe0), ENDS_ONE)
    d[3] = forward(3, d[2])
    x3 = swap("c3", after(p3, x2), CENTRES)
    pe3 = part("e3", el[0], at_end(3))
    xe3 = swap("e3", after(pe3, xe2), ENDS_ONE)

    u0 = total("cu0", cut(at_centre[0], x), at_centre[0], xu0)
    v0 = total("cv0", cut(centre_v, x), at_centre[0], xv0)
    by_centre = [
        jnp.concatenate([u0, v0], 0),
        total("c1", cl[1], at_centre[1], x1),
        total("c2", cl[1], at_centre[2], x2),
        total("c3", cl[1], at_centre[3], x3),
    ]
    near_end = total("e0", el[1], near, xe0)
    by_end = [
        near_end[:, :group],
        near_end[:, group:],
        total("e2", el[1], at_end(2), xe2),
        total("e3", el[1], at_end(3), xe3),
    ]

    targets = target_product.shape[1]
    half_targets = targets // 2

    def partial_scores(which):
        t = lax.dynamic_slice_in_dim(target_product, which * half_targets, half_targets, 1)
        return jnp.concatenate(
            [jnp.dot(s, t, preferred_element_type=jnp.float32) for s in (slab_one, slab_two)], 0
        )

    with jax.named_scope("scores"):
        other_scores = swap_core(after(partial_scores(1 - core), c[0]))
    scores = (partial_scores(core) + other_scores).astype(jnp.bfloat16)
    scores = scores.reshape(2, row_count, half_targets)

    def finish(ks):
        result = jnp.concatenate(
            [jnp.where(centre, by_centre[k], by_end[k]) for k in ks], 1
        )
        with jax.named_scope("end_diag"):
            end_diag = permute(result[block:], on_core(0, OUT))
        with jax.named_scope("low_cross"):
            low_cross = lax.ppermute(result[block : block + block // 2], "feat", [(1, 0)])
        diag = jnp.where((core == 0) & ~centre, end_diag, result[:block])
        cross = jnp.where(core == 0, low_cross, result[block + block // 2 :])
        return [
            [v[:, i * group : (i + 1) * group] for i in range(len(ks))] for v in (diag, cross)
        ]

    first, last = finish((0, 1, 2)), finish((3,))

    def assemble(p):
        p = [p[1], p[0], p[2], p[3]]
        return jnp.concatenate([jnp.where(lower, p[i], p[3 - i]) for i in range(4)], 1)

    kernel_diag = assemble(first[0] + last[0])[None]
    kernel_cross = assemble(first[1] + last[1])
    return (kernel_diag, kernel_cross, scores)


def solution(mesh):
    in_specs = (P(("grp", "ex"), "feat"), P(("grp", "ex"), "feat"), P("feat", "grp"))
    out_specs = (
        P("feat", ("grp", "ex"), None),
        P(("grp", "ex", "feat"), None),
        P(None, ("grp", "ex"), "feat"),
    )
    few = mesh.shape["ex"] == Z * X and mesh.shape["feat"] == 2
    return jax.shard_map(
        gathering if few else reducing,
        mesh=mesh,
        in_specs=in_specs,
        out_specs=out_specs,
        check_vma=False,
    )
```

time: 489 us -> 200 us (0.41)
  waiting for transfers between devices: 417 us -> 76.7 us
  starting transfers between devices: 0.16 us -> 54.2 us
  matrix products: 22 us -> 40.5 us
  other arithmetic: 0.84 us -> 16.5 us
  local copies, waits for them, and re-layouts: 22.3 us -> 9.71 us
  between operations: 13.9 us -> 1.62 us
  blocking collectives: 11.8 us -> 0 us
    reduce_scatter x2 -> x0, waiting for transfers between devices: 393 us -> none  [per_device(): lax.psum_scatter(total * factor, 'ex', scatter_dimension=0, tiled=True)]
    ppermute x0 -> x29, waiting for transfers between devices: none -> 76.7 us  [the longest x17 49.5 us: permute(): return lax.ppermute(value, ('ex', 'feat'), pairs)]
    ppermute x0 -> x29, starting transfers between devices: none -> 54.2 us  [the longest x17 42.2 us: permute(): return lax.ppermute(value, ('ex', 'feat'), pairs)]
    all_gather x2 -> x0, waiting for transfers between devices: 23.9 us -> none  [the longest x1 12.4 us: per_device(): lax.all_gather(slab_two, 'feat', axis=1, tiled=True)]
    dot_general x4 -> x16, matrix products: 16.9 us -> 29.1 us  [gram_part(): lax.dot_general(left, right, (((0,), (0,)), ((), ())), preferred_element_...]
    all_to_all x1 -> x0, blocking collectives: 11.8 us -> none  [per_device(): lax.all_to_all(target_product, 'feat', split_axis=1, concat_axis=0, tiled...]
    concatenate x0 -> x15, other arithmetic: none -> 10.2 us  [the longest x3 2.55 us: own(): jnp.concatenate([lax.dynamic_slice_in_dim(s, start, group, 1) for s in (s...]
    all_to_all x1 -> x0, local copies, waits for them, and re-layouts: 6.46 us -> none  [per_device(): lax.all_to_all(target_product, 'feat', split_axis=1, concat_axis=0, tiled...]
  transfers between devices with their start and end apart: 4 -> 29, of which waited for: 4 -> 8; matrix products, arithmetic and copies ran while one was open for 7% -> 28% of each run, Pallas kernels for 0% -> 0%
where the time goes in v2:
time: 200 us; the launch traced here: 199 us
  waiting for transfers between devices  76.7 us (38%)
  starting transfers between devices  54.2 us (27%)
  matrix products  40.5 us (20%)
  other arithmetic  16.5 us (8%)
  local copies, waits for them, and re-layouts  9.71 us (5%)
    ppermute x17, waiting for transfers between devices, permute(): return lax.ppermute(value, ('ex', 'feat'), pairs)  49.5 us
    ppermute x17, starting transfers between devices, permute(): return lax.ppermute(value, ('ex', 'feat'), pairs)  42.2 us
    dot_general x16, matrix products, gram_part(): lax.dot_general(left, right, (((0,), (0,)), ((), ())), preferred_element_...  29.1 us
    ppermute x2, waiting for transfers between devices, finish(): low_cross = lax.ppermute(result[block:block + block // 2], 'feat', [(1, 0)])  27.2 us
    dot_general x4, matrix products, partial_scores(): jnp.dot(s, t, preferred_element_type=jnp.float32)  11.3 us
    unnamed x67, local copies, waits for them, and re-layouts  7.13 us
    ppermute x8, starting transfers between devices, swap_x(): return lax.ppermute(value, ('ex', 'feat'), pairs)  6.75 us
  transfers between devices with their start and end apart: 29, of which 8 were waited for; matrix products, arithmetic and copies ran while one was open for 28% of the time, Pallas kernels for 0%

profile of v2, /device:TPU:0, one launch (start us, length us, event | category | flops | bytes accessed | tf_op | source)
XLA Modules:
  0.0 199.3 jit_solution(13067215392199439649)
XLA Ops:
  0.7 1.7 constant_dynamic-slice_fusion.12
  2.4 0.9 pad_maximum_fusion.29
  3.3 1.4 collective-permute-start.1
  4.8 6.9 %collective-permute-start.2 = (bf16[512,512]{1,0:T(8,128)(2,1)}, bf16[512,512]{1,0:T(8,128)(2,1)S(1)}, u32[]{:S(2)}, u32[]{:S(2)}) collective-permute-start(bf16[512,512]{1,0:T(8,128)(2,1)} %pad_maximum_fusion.29), channel_id=1, source_target_pairs={{0,8},{2,10},{12,4},{14,6},{1,9},{3,11},{13,5},{15,7},{16,24},{18,... | collective-permute-start | bytes 1572872 | tf_op jit(solution)/shard_map/over0/ppermute | solution.py:59
  11.7 1.1 maximum_maximum_fusion.1
  12.8 2.4 %collective-permute-start = (bf16[512,1024]{1,0:T(8,128)(2,1)}, bf16[512,1024]{1,0:T(8,128)(2,1)}, u32[]{:S(2)}, u32[]{:S(2)}) collective-permute-start(bf16[512,1024]{1,0:T(8,128)(2,1)} %maximum_maximum_fusion.1), channel_id=1, source_target_pairs={{0,4},{2,6},{12,8},{14,10},{1,5},{3,7},{13,9},{15,11},{5,1},{7,3},... | collective-permute-start | bytes 3145736 | tf_op jit(solution)/shard_map/half0/ppermute | solution.py:59
  15.2 1.1 maximum_maximum_fusion.2
  16.3 3.5 %fusion.24 = f32[256,512]{1,0:T(8,128)} fusion(bf16[256,2048]{1,0:T(8,128)(2,1)} %param.4, bf16[2048,1024]{1,0:T(8,128)(2,1)} %param.5, s32[]{:T(128)S(6)} %select_n.203), kind=kOutput, calls=%fused_computation.45 | convolution fusion | flops 536870912 | bytes 3670020 | tf_op jit(solution)/shard_map/scores/dot_general | solution.py:230
  19.8 0.8 pad_maximum_fusion.30
  20.7 3.2 %fusion.27 = f32[256,512]{1,0:T(8,128)} fusion(bf16[256,2048]{1,0:T(8,128)(2,1)S(1)} %copy-done.14, bf16[2048,1024]{1,0:T(8,128)(2,1)} %param.5, s32[]{:T(128)S(6)} %select_n.203), kind=kOutput, calls=%fused_computation.46 | convolution fusion | flops 536870912 | bytes 3670020 | tf_op jit(solution)/shard_map/scores/dot_general | solution.py:230
  23.9 3.1 %fusion.18 = f32[256,512]{1,0:T(8,128)} fusion(bf16[256,2048]{1,0:T(8,128)(2,1)S(1)} %copy-done.13, bf16[2048,1024]{1,0:T(8,128)(2,1)} %param.5, s32[]{:T(128)S(6)} %select_n.202), kind=kOutput, calls=%fused_computation.43 | convolution fusion | flops 536870912 | bytes 3670020 | tf_op jit(solution)/shard_map/dot_general | solution.py:230
  27.0 1.5 fusion.21
  29.2 2.1 %pad_maximum_fusion.10 = bf16[1024,512]{1,0:T(8,128)(2,1)} fusion(bf16[512,512]{1,0:T(8,128)(2,1)S(1)} %collective-permute-done.2, bf16[512,512]{1,0:T(8,128)(2,1)} %collective-permute-done.1), kind=kLoop, calls=%fused_computation.52 | loop fusion | flops 2097152 | bytes 2097152 | tf_op jit(solution)/shard_map/concatenate | solution.py:133
  31.3 1.7 collective-permute-start.8
  33.0 12.4 %collective-permute-done = bf16[512,1024]{1,0:T(8,128)(2,1)} collective-permute-done((bf16[512,1024]{1,0:T(8,128)(2,1)}, bf16[512,1024]{1,0:T(8,128)(2,1)}, u32[]{:S(2)}, u32[]{:S(2)}) %collective-permute-start) | collective-permute-done | bytes 1048608 | tf_op jit(solution)/shard_map/half0/ppermute | solution.py:59
  45.3 2.7 %fusion.55 = (bf16[512,512]{1,0:T(8,128)(2,1)}, bf16[2048,512]{1,0:T(8,128)(2,1)S(1)}, bf16[2048,512]{1,0:T(8,128)(2,1)S(1)}, bf16[2048,512]{1,0:T(8,128)(2,1)},...) fusion(bf16[512,1024]{1,0:T(8,128)(2,1)} %collective-permute-done, bf16[256,512]{1,0:T(8,128)(2,1)S(1)} %get-tuple-element.69, ...), kind=kLoop, calls=%fused_computation.136 | loop fusion | flops 1310717 | bytes 4718593 | tf_op jit(solution)/shard_map/slice | solution.py:130
  48.1 1.1 constant_dynamic-update-slice_fusion.11
  49.3 1.3 copy-done.20
  50.8 1.2 copy-done.7
  52.0 1.5 fusion.56
  53.5 5.4 %collective-permute-start.5 = (bf16[512,512]{1,0:T(8,128)(2,1)}, bf16[512,512]{1,0:T(8,128)(2,1)S(1)}, u32[]{:S(2)}, u32[]{:S(2)}) collective-permute-start(bf16[512,512]{1,0:T(8,128)(2,1)} %pad_maximum_fusion.30), channel_id=1, source_target_pairs={{0,8},{2,10},{12,4},{14,6},{1,9},{3,11},{13,5},{15,7},{16,24},{18,... | collective-permute-start | bytes 1572872 | tf_op jit(solution)/shard_map/over1/ppermute | solution.py:59
  59.0 0.8 pad_maximum_fusion.27
  59.8 1.4 pad_maximum_fusion.14
  62.1 2.5 %collective-permute-start.6 = (bf16[2048,512]{1,0:T(8,128)(2,1)}, bf16[2048,512]{1,0:T(8,128)(2,1)S(1)}, u32[]{:S(2)}, u32[]{:S(2)}) collective-permute-start(bf16[2048,512]{1,0:T(8,128)(2,1)} %copy-done.20), channel_id=1, source_target_pairs={{0,1},{2,3},{4,5},{6,7},{8,9},{10,11},{12,13},{14,15},{16,17},{18,... | collective-permute-start | bytes 6291464 | tf_op jit(solution)/shard_map/across/ppermute | solution.py:164
  64.7 2.7 %collective-permute-start.13 = (bf16[512,1024]{1,0:T(8,128)(2,1)S(1)}, bf16[512,1024]{1,0:T(8,128)(2,1)S(1)}, u32[]{:S(2)}, u32[]{:S(2)}) collective-permute-start(bf16[512,1024]{1,0:T(8,128)(2,1)S(1)} %copy-done.12), channel_id=1, source_target_pairs={{0,4},{2,6},{12,8},{14,10},{1,5},{3,7},{13,9},{15,11},{5,1},{7,3},... | collective-permute-start | bytes 3145736 | tf_op jit(solution)/shard_map/half2/ppermute | solution.py:59
  67.4 4.2 %collective-permute-done.5 = bf16[512,512]{1,0:T(8,128)(2,1)S(1)} collective-permute-done((bf16[512,512]{1,0:T(8,128)(2,1)}, bf16[512,512]{1,0:T(8,128)(2,1)S(1)}, u32[]{:S(2)}, u32[]{:S(2)}) %collective-permute-start.5) | collective-permute-done | bytes 524320 | tf_op jit(solution)/shard_map/over1/ppermute | solution.py:59
  71.7 0.9 collective-permute-start.9
  72.7 0.8 collective-permute-start.10
  75.2 0.9 fusion.32
  76.2 15.4 %collective-permute-done.13 = bf16[512,1024]{1,0:T(8,128)(2,1)S(1)} collective-permute-done((bf16[512,1024]{1,0:T(8,128)(2,1)S(1)}, bf16[512,1024]{1,0:T(8,128)(2,1)S(1)}, u32[]{:S(2)}, u32[]{:S(2)}) %collective-permute-start.13) | collective-permute-done | bytes 1048608 | tf_op jit(solution)/shard_map/half2/ppermute | solution.py:59
  92.0 0.8 copy-done.9
  95.0 1.3 fusion.35
  96.3 0.7 collective-permute-start.12
  97.1 8.7 %collective-permute-start.15 = (bf16[512,512]{1,0:T(8,128)(2,1)S(1)}, bf16[512,512]{1,0:T(8,128)(2,1)S(1)}, u32[]{:S(2)}, u32[]{:S(2)}) collective-permute-start(bf16[512,512]{1,0:T(8,128)(2,1)S(1)} %copy-done.19), channel_id=1, source_target_pairs={{0,8},{2,10},{12,4},{14,6},{1,9},{3,11},{13,5},{15,7},{16,24},{18,... | collective-permute-start | bytes 1572872 | tf_op jit(solution)/shard_map/over2/ppermute | solution.py:59
  106.0 0.9 copy-done.15
  106.9 4.9 %fusion.38 = f32[512,1024]{1,0:T(8,128)} fusion(bf16[2048,256]{1,0:T(8,128)(2,1)S(1)} %get-tuple-element.50, bf16[2048,256]{1,0:T(8,128)(2,1)S(1)} %get-tuple-element.48, bf16[1024,512]{1,0:T(8,128)(2,1)S(1)} %collective-permute-done.9, bf16[512,512]{1,0:T(8,128)(2,1)S(1)} %copy-done.9, bf16[256,512]{1,0:T(8,128)(2,1)S(1)} %get-tuple-element.69, ...), kind=kOutput, calls=%fused_computation.66 | convolution fusion | flops 2185232384 | bytes 8388608 | tf_op jit(solution)/shard_map/e0/dot_general | solution.py:10
  111.8 0.8 collective-permute-start.11
  113.4 1.3 fusion.34
  114.7 5.2 %collective-permute-start.21 = (bf16[512,512]{1,0:T(8,128)(2,1)S(1)}, bf16[512,512]{1,0:T(8,128)(2,1)S(1)}, u32[]{:S(2)}, u32[]{:S(2)}) collective-permute-start(bf16[512,512]{1,0:T(8,128)(2,1)S(1)} %copy-done.16), channel_id=1, source_target_pairs={{0,8},{2,10},{12,4},{14,6},{1,9},{3,11},{13,5},{15,7},{16,24},{18,... | collective-permute-start | bytes 1572872 | tf_op jit(solution)/shard_map/over3/ppermute | solution.py:59
  119.9 0.7 collective-permute-start.17
  121.4 0.7 collective-permute-start.16
  122.2 4.5 %collective-permute-done.21 = bf16[512,512]{1,0:T(8,128)(2,1)S(1)} collective-permute-done((bf16[512,512]{1,0:T(8,128)(2,1)S(1)}, bf16[512,512]{1,0:T(8,128)(2,1)S(1)}, u32[]{:S(2)}, u32[]{:S(2)}) %collective-permute-start.21) | collective-permute-done | bytes 524320 | tf_op jit(solution)/shard_map/over3/ppermute | solution.py:59
  126.9 1.3 fusion.33
  128.2 0.7 collective-permute-start.23
  128.9 2.2 %fusion.37 = f32[512,512]{1,0:T(8,128)} fusion(bf16[2048,256]{1,0:T(8,128)(2,1)S(1)} %get-tuple-element.50, bf16[2048,256]{1,0:T(8,128)(2,1)S(1)} %get-tuple-element.48, bf16[1024,512]{1,0:T(8,128)(2,1)S(1)} %collective-permute-done.17, bf16[512,512]{1,0:T(8,128)(2,1)S(1)} %get-tuple-element.56, bf16[256,512]{1,0:T(8,128)(2,1)S(1)} %copy-done.3, ...), kind=kOutput, calls=%fused_computation.65 | convolution fusion | flops 1086324736 | bytes 5242880 | tf_op jit(solution)/shard_map/e2/dot_general | solution.py:10
  131.1 1.7 collective-permute-start.18
  133.6 4.3 %add_multiply_fusion = f32[512,1024]{1,0:T(8,128)S(1)} fusion(f32[512,1024]{1,0:T(8,128)} %copy-done.22, bf16[2048,256]{1,0:T(8,128)(2,1)S(1)} %get-tuple-element.49, bf16[2048,256]{1,0:T(8,128)(2,1)S(1)} %get-tuple-element.47, bf16[1024,512]{1,0:T(8,128)(2,1)S(1)} %collective-permute-done.9, bf16[512,512]{1,0:T(8,128)(2,1)S(1)} %copy-done.9, ...), kind=kOutput, calls=%fused_computation.14 | convolution fusion | flops 2186280960 | bytes 10485760 | tf_op jit(solution)/shard_map/e0/dot_general | solution.py:10
  138.0 1.3 fusion.15
  139.4 1.0 copy-done.25
  140.3 2.6 %fusion.36 = f32[512,512]{1,0:T(8,128)S(1)} fusion(bf16[2048,256]{1,0:T(8,128)(2,1)S(1)} %get-tuple-element.50, bf16[2048,256]{1,0:T(8,128)(2,1)S(1)} %get-tuple-element.48, bf16[1024,512]{1,0:T(8,128)(2,1)} %copy-done.25, bf16[512,512]{1,0:T(8,128)(2,1)S(1)} %get-tuple-element.55, bf16[256,512]{1,0:T(8,128)(2,1)S(1)} %get-tuple-element.67, ...), kind=kOutput, calls=%fused_computation.64 | convolution fusion | flops 1086324736 | bytes 5242880 | tf_op jit(solution)/shard_map/e3/dot_general | solution.py:10
  143.7 2.5 %fusion.11 = f32[512,512]{1,0:T(8,128)S(1)} fusion(f32[512,512]{1,0:T(8,128)} %collective-permute-done.18, bf16[2048,256]{1,0:T(8,128)(2,1)S(1)} %get-tuple-element.49, bf16[2048,256]{1,0:T(8,128)(2,1)S(1)} %get-tuple-element.47, bf16[1024,512]{1,0:T(8,128)(2,1)S(1)} %copy-done.24, bf16[512,512]{1,0:T(8,128)(2,1)S(1)} %get-tuple-element.56, ...), kind=kOutput, calls=%fused_computation.32 | convolution fusion | flops 1086849024 | bytes 6291456 | tf_op jit(solution)/shard_map/e2/dot_general | solution.py:10
  146.2 1.3 fusion.13
  147.8 1.4 collective-permute-start.26
  149.3 1.3 collective-permute-start.19
  150.6 1.3 fusion.8
  151.9 1.3 fusion.10
  153.2 1.3 collective-permute-start.27
  154.5 18.4 %collective-permute-done.26 = f32[128,1536]{1,0:T(8,128)S(1)} collective-permute-done((f32[128,1536]{1,0:T(8,128)S(1)}, f32[128,1536]{1,0:T(8,128)S(1)}, u32[]{:S(2)}, u32[]{:S(2)}) %collective-permute-start.26) | collective-permute-done | bytes 786464 | tf_op jit(solution)/shard_map/low_cross/ppermute | solution.py:245
  173.0 1.3 collective-permute-start.25
  174.3 8.8 %collective-permute-done.27 = f32[128,512]{1,0:T(8,128)S(1)} collective-permute-done((f32[128,512]{1,0:T(8,128)S(1)}, f32[128,512]{1,0:T(8,128)S(1)}, u32[]{:S(2)}, u32[]{:S(2)}) %collective-permute-start.27) | collective-permute-done | bytes 262176 | tf_op jit(solution)/shard_map/low_cross/ppermute | solution.py:245
  183.3 1.0 pad_maximum_fusion.13
  184.3 7.5 %collective-permute-done.19 = f32[256,1536]{1,0:T(8,128)S(1)} collective-permute-done((f32[256,1536]{1,0:T(8,128)S(1)}, f32[256,1536]{1,0:T(8,128)S(1)}, u32[]{:S(2)}, u32[]{:S(2)}) %collective-permute-start.19) | collective-permute-done | bytes 1572896 | tf_op jit(solution)/shard_map/end_diag/ppermute | solution.py:59
  192.0 5.4 %collective-permute-done.25 = f32[256,512]{1,0:T(8,128)S(1)} collective-permute-done((f32[256,512]{1,0:T(8,128)S(1)}, f32[256,512]{1,0:T(8,128)S(1)}, u32[]{:S(2)}, u32[]{:S(2)}) %collective-permute-start.25) | collective-permute-done | bytes 524320 | tf_op jit(solution)/shard_map/end_diag/ppermute | solution.py:59
  197.8 1.5 maximum_bitcast_fusion
  (118 shorter events, 10.9 us)
Async XLA Ops:
  2.4 13.9 %copy-start.2 = (bf16[256,512]{1,0:T(8,128)(2,1)}, bf16[256,512]{1,0:T(8,128)(2,1)S(1)}, u32[]{:S(2)}) copy-start(bf16[256,512]{1,0:T(8,128)(2,1)S(1)} %get-tuple-element.68) | copy-start | bytes 786436
  2.4 13.9 %copy-start.4 = (bf16[256,512]{1,0:T(8,128)(2,1)}, bf16[256,512]{1,0:T(8,128)(2,1)S(1)}, u32[]{:S(2)}) copy-start(bf16[256,512]{1,0:T(8,128)(2,1)S(1)} %get-tuple-element.82) | copy-start | bytes 786436
  2.4 17.4 %copy-start = (bf16[256,512]{1,0:T(8,128)(2,1)}, bf16[256,512]{1,0:T(8,128)(2,1)S(1)}, u32[]{:S(2)}) copy-start(bf16[256,512]{1,0:T(8,128)(2,1)S(1)} %get-tuple-element.83) | copy-start | bytes 786436
  3.3 25.2 %collective-permute-start.1 = (bf16[512,512]{1,0:T(8,128)(2,1)}, bf16[512,512]{1,0:T(8,128)(2,1)}, u32[]{:S(2)}, u32[]{:S(2)}) collective-permute-start(bf16[512,512]{1,0:T(8,128)(2,1)} %pad_maximum_fusion.29), channel_id=1, source_target_pairs={{4,8},{6,10},{8,4},{10,6},{5,9},{7,11},{9,5},{11,7},{20,24},{22,26... | collective-permute-start | bytes 1572872 | tf_op jit(solution)/shard_map/middle0/ppermute | solution.py:59
  4.8 24.4 %collective-permute-start.2 = (bf16[512,512]{1,0:T(8,128)(2,1)}, bf16[512,512]{1,0:T(8,128)(2,1)S(1)}, u32[]{:S(2)}, u32[]{:S(2)}) collective-permute-start(bf16[512,512]{1,0:T(8,128)(2,1)} %pad_maximum_fusion.29), channel_id=1, source_target_pairs={{0,8},{2,10},{12,4},{14,6},{1,9},{3,11},{13,5},{15,7},{16,24},{18,... | collective-permute-start | bytes 1572872 | tf_op jit(solution)/shard_map/over0/ppermute | solution.py:59
  12.8 32.6 %collective-permute-start = (bf16[512,1024]{1,0:T(8,128)(2,1)}, bf16[512,1024]{1,0:T(8,128)(2,1)}, u32[]{:S(2)}, u32[]{:S(2)}) collective-permute-start(bf16[512,1024]{1,0:T(8,128)(2,1)} %maximum_maximum_fusion.1), channel_id=1, source_target_pairs={{0,4},{2,6},{12,8},{14,10},{1,5},{3,7},{13,9},{15,11},{5,1},{7,3},... | collective-permute-start | bytes 3145736 | tf_op jit(solution)/shard_map/half0/ppermute | solution.py:59
  16.3 4.3 %copy-start.14 = (bf16[256,2048]{1,0:T(8,128)(2,1)S(1)}, bf16[256,2048]{1,0:T(8,128)(2,1)}, u32[]{:S(2)}) copy-start(bf16[256,2048]{1,0:T(8,128)(2,1)} %param.3) | copy-start | bytes 3145732
  20.7 3.2 %copy-start.13 = (bf16[256,2048]{1,0:T(8,128)(2,1)S(1)}, bf16[256,2048]{1,0:T(8,128)(2,1)}, u32[]{:S(2)}) copy-start(bf16[256,2048]{1,0:T(8,128)(2,1)} %param.4) | copy-start | bytes 3145732
  20.7 6.3 %copy-start.21 = (bf16[2048,1024]{1,0:T(8,128)(2,1)S(1)}, bf16[2048,1024]{1,0:T(8,128)(2,1)}, u32[]{:S(2)}) copy-start(bf16[2048,1024]{1,0:T(8,128)(2,1)} %param.5) | copy-start | bytes 12582916
  28.5 33.6 %collective-permute-start.4 = (bf16[512,512]{1,0:T(8,128)(2,1)}, bf16[512,512]{1,0:T(8,128)(2,1)S(1)}, u32[]{:S(2)}, u32[]{:S(2)}) collective-permute-start(bf16[512,512]{1,0:T(8,128)(2,1)} %pad_maximum_fusion.30), channel_id=1, source_target_pairs={{4,8},{6,10},{8,4},{10,6},{5,9},{7,11},{9,5},{11,7},{20,24},{22,26... | collective-permute-start | bytes 1572872 | tf_op jit(solution)/shard_map/middle1/ppermute | solution.py:59
  31.3 33.4 %collective-permute-start.8 = (bf16[1024,512]{1,0:T(8,128)(2,1)}, bf16[1024,512]{1,0:T(8,128)(2,1)}, u32[]{:S(2)}, u32[]{:S(2)}) collective-permute-start(bf16[1024,512]{1,0:T(8,128)(2,1)} %pad_maximum_fusion.10), channel_id=1, source_target_pairs={{5,1},{7,3},{9,13},{11,15},{21,17},{23,19},{25,29},{27,31}} | collective-permute-start | bytes 3145736 | tf_op jit(solution)/shard_map/forward0/ppermute | solution.py:59
  49.3 1.3 copy-start.20
  50.7 1.3 copy-start.7
  50.8 2.7 %copy-start.10 = (bf16[2048,256]{1,0:T(8,128)(2,1)}, bf16[2048,256]{1,0:T(8,128)(2,1)S(1)}, u32[]{:S(2)}) copy-start(bf16[2048,256]{1,0:T(8,128)(2,1)S(1)} %get-tuple-element.44) | copy-start | bytes 3145732
  53.5 18.1 %collective-permute-start.5 = (bf16[512,512]{1,0:T(8,128)(2,1)}, bf16[512,512]{1,0:T(8,128)(2,1)S(1)}, u32[]{:S(2)}, u32[]{:S(2)}) collective-permute-start(bf16[512,512]{1,0:T(8,128)(2,1)} %pad_maximum_fusion.30), channel_id=1, source_target_pairs={{0,8},{2,10},{12,4},{14,6},{1,9},{3,11},{13,5},{15,7},{16,24},{18,... | collective-permute-start | bytes 1572872 | tf_op jit(solution)/shard_map/over1/ppermute | solution.py:59
  59.8 2.2 %copy-start.6 = (bf16[2048,512]{1,0:T(8,128)(2,1)S(1)}, bf16[2048,512]{1,0:T(8,128)(2,1)}, u32[]{:S(2)}) copy-start(bf16[2048,512]{1,0:T(8,128)(2,1)} %get-tuple-element.60) | copy-start | bytes 6291460
  59.8 4.9 %copy-start.12 = (bf16[512,1024]{1,0:T(8,128)(2,1)S(1)}, bf16[512,1024]{1,0:T(8,128)(2,1)}, u32[]{:S(2)}) copy-start(bf16[512,1024]{1,0:T(8,128)(2,1)} %maximum_maximum_fusion.2) | copy-start | bytes 3145732
  61.2 13.0 %collective-permute-start.28 = (f32[512,512]{1,0:T(8,128)S(1)}, f32[512,512]{1,0:T(8,128)S(1)}, u32[]{:S(2)}, u32[]{:S(2)}) collective-permute-start(f32[512,512]{1,0:T(8,128)S(1)} %pad_maximum_fusion.14), channel_id=1, source_target_pairs={{0,1},{1,0},{2,3},{3,2},{4,5},{5,4},{6,7},{7,6},{8,9},{9,8},{10,11... | collective-permute-start | bytes 3145736 | tf_op jit(solution)/shard_map/scores/ppermute | solution.py:70
  61.3 11.4 %collective-permute-start.3 = (f32[256,512]{1,0:T(8,128)}, f32[256,512]{1,0:T(8,128)S(1)}, u32[]{:S(2)}, u32[]{:S(2)}) collective-permute-start(f32[256,512]{1,0:T(8,128)} %fusion.56), channel_id=1, source_target_pairs={{4,6},{6,4},{5,7},{7,5},{8,10},{10,8},{9,11},{11,9},{20,22},{22,20... | collective-permute-start | bytes 1572872 | tf_op jit(solution)/shard_map/cu0/ppermute | solution.py:66
  62.1 31.1 %collective-permute-start.6 = (bf16[2048,512]{1,0:T(8,128)(2,1)}, bf16[2048,512]{1,0:T(8,128)(2,1)S(1)}, u32[]{:S(2)}, u32[]{:S(2)}) collective-permute-start(bf16[2048,512]{1,0:T(8,128)(2,1)} %copy-done.20), channel_id=1, source_target_pairs={{0,1},{2,3},{4,5},{6,7},{8,9},{10,11},{12,13},{14,15},{16,17},{18,... | collective-permute-start | bytes 6291464 | tf_op jit(solution)/shard_map/across/ppermute | solution.py:164
  64.7 27.0 %collective-permute-start.13 = (bf16[512,1024]{1,0:T(8,128)(2,1)S(1)}, bf16[512,1024]{1,0:T(8,128)(2,1)S(1)}, u32[]{:S(2)}, u32[]{:S(2)}) collective-permute-start(bf16[512,1024]{1,0:T(8,128)(2,1)S(1)} %copy-done.12), channel_id=1, source_target_pairs={{0,4},{2,6},{12,8},{14,10},{1,5},{3,7},{13,9},{15,11},{5,1},{7,3},... | collective-permute-start | bytes 3145736 | tf_op jit(solution)/shard_map/half2/ppermute | solution.py:59
  71.7 1.8 copy-start.8
  71.7 20.3 %collective-permute-start.9 = (bf16[1024,512]{1,0:T(8,128)(2,1)S(1)}, bf16[1024,512]{1,0:T(8,128)(2,1)S(1)}, u32[]{:S(2)}, u32[]{:S(2)}) collective-permute-start(bf16[1024,512]{1,0:T(8,128)(2,1)S(1)} %pad_maximum_fusion.9), channel_id=1, source_target_pairs={{5,1},{7,3},{9,13},{11,15},{21,17},{23,19},{25,29},{27,31}} | collective-permute-start | bytes 3145736 | tf_op jit(solution)/shard_map/forward1/ppermute | solution.py:59
  72.7 33.1 %collective-permute-start.10 = (bf16[1536,512]{1,0:T(8,128)(2,1)S(1)}, bf16[1536,512]{1,0:T(8,128)(2,1)S(1)}, u32[]{:S(2)}, u32[]{:S(2)}) collective-permute-start(bf16[1536,512]{1,0:T(8,128)(2,1)S(1)} %pad_maximum_fusion.8), channel_id=1, source_target_pairs={{4,1},{6,3},{8,13},{10,15},{20,17},{22,19},{24,29},{26,31}} | collective-permute-start | bytes 4718600 | tf_op jit(solution)/shard_map/given/ppermute | solution.py:59
  73.5 1.0 copy-start.19
  73.5 1.7 copy-start.17
  73.5 1.7 copy-start.18
  74.5 17.5 %collective-permute-start.14 = (bf16[512,512]{1,0:T(8,128)(2,1)S(1)}, bf16[512,512]{1,0:T(8,128)(2,1)S(1)}, u32[]{:S(2)}, u32[]{:S(2)}) collective-permute-start(bf16[512,512]{1,0:T(8,128)(2,1)S(1)} %copy-done.19), channel_id=1, source_target_pairs={{4,8},{6,10},{8,4},{10,6},{5,9},{7,11},{9,5},{11,7},{20,24},{22,26... | collective-permute-start | bytes 1572872 | tf_op jit(solution)/shard_map/middle2/ppermute | solution.py:59
  76.2 15.7 %copy-start.5 = (bf16[256,512]{1,0:T(8,128)(2,1)S(1)}, bf16[256,512]{1,0:T(8,128)(2,1)}, u32[]{:S(2)}) copy-start(bf16[256,512]{1,0:T(8,128)(2,1)} %copy-done.4) | copy-start | bytes 786436
  76.2 15.7 %copy-start.3 = (bf16[256,512]{1,0:T(8,128)(2,1)S(1)}, bf16[256,512]{1,0:T(8,128)(2,1)}, u32[]{:S(2)}) copy-start(bf16[256,512]{1,0:T(8,128)(2,1)} %copy-done.2) | copy-start | bytes 786436
  76.2 15.7 %copy-start.1 = (bf16[256,512]{1,0:T(8,128)(2,1)S(1)}, bf16[256,512]{1,0:T(8,128)(2,1)}, u32[]{:S(2)}) copy-start(bf16[256,512]{1,0:T(8,128)(2,1)} %copy-done) | copy-start | bytes 786436
  91.8 1.0 copy-start.9
  93.6 1.4 copy-start.11
  94.3 18.3 %collective-permute-start.7 = (f32[256,512]{1,0:T(8,128)S(1)}, f32[256,512]{1,0:T(8,128)S(1)}, u32[]{:S(2)}, u32[]{:S(2)}) collective-permute-start(f32[256,512]{1,0:T(8,128)S(1)} %fusion.57), channel_id=1, source_target_pairs={{4,6},{6,4},{5,7},{7,5},{8,10},{10,8},{9,11},{11,9},{20,22},{22,20... | collective-permute-start | bytes 1572872 | tf_op jit(solution)/shard_map/cv0/ppermute | solution.py:66
  96.3 25.1 %collective-permute-start.12 = (f32[512,512]{1,0:T(8,128)S(1)}, f32[512,512]{1,0:T(8,128)S(1)}, u32[]{:S(2)}, u32[]{:S(2)}) collective-permute-start(f32[512,512]{1,0:T(8,128)S(1)} %fusion.35), channel_id=1, source_target_pairs={{4,6},{6,4},{5,7},{7,5},{8,10},{10,8},{9,11},{11,9},{20,22},{22,20... | collective-permute-start | bytes 3145736 | tf_op jit(solution)/shard_map/c1/ppermute | solution.py:66
  97.1 16.3 %collective-permute-start.15 = (bf16[512,512]{1,0:T(8,128)(2,1)S(1)}, bf16[512,512]{1,0:T(8,128)(2,1)S(1)}, u32[]{:S(2)}, u32[]{:S(2)}) collective-permute-start(bf16[512,512]{1,0:T(8,128)(2,1)S(1)} %copy-done.19), channel_id=1, source_target_pairs={{0,8},{2,10},{12,4},{14,6},{1,9},{3,11},{13,5},{15,7},{16,24},{18,... | collective-permute-start | bytes 1572872 | tf_op jit(solution)/shard_map/over2/ppermute | solution.py:59
  105.8 1.0 copy-start.15
  106.9 5.8 %copy-start.16 = (bf16[512,512]{1,0:T(8,128)(2,1)S(1)}, bf16[512,512]{1,0:T(8,128)(2,1)}, u32[]{:S(2)}) copy-start(bf16[512,512]{1,0:T(8,128)(2,1)} %get-tuple-element.32) | copy-start | bytes 1572868
  111.8 19.3 %collective-permute-start.11 = (f32[512,1024]{1,0:T(8,128)}, f32[512,1024]{1,0:T(8,128)S(1)}, u32[]{:S(2)}, u32[]{:S(2)}) collective-permute-start(f32[512,1024]{1,0:T(8,128)} %fusion.38), channel_id=1, source_target_pairs={{1,3},{3,1},{13,15},{15,13},{17,19},{19,17},{29,31},{31,29}} | collective-permute-start | bytes 6291464 | tf_op jit(solution)/shard_map/e0/ppermute | solution.py:66
  112.6 9.5 %collective-permute-start.20 = (bf16[512,512]{1,0:T(8,128)(2,1)S(1)}, bf16[512,512]{1,0:T(8,128)(2,1)S(1)}, u32[]{:S(2)}, u32[]{:S(2)}) collective-permute-start(bf16[512,512]{1,0:T(8,128)(2,1)S(1)} %copy-done.16), channel_id=1, source_target_pairs={{4,8},{6,10},{8,4},{10,6},{5,9},{7,11},{9,5},{11,7},{20,24},{22,26... | collective-permute-start | bytes 1572872 | tf_op jit(solution)/shard_map/middle3/ppermute | solution.py:59
  114.7 12.1 %collective-permute-start.21 = (bf16[512,512]{1,0:T(8,128)(2,1)S(1)}, bf16[512,512]{1,0:T(8,128)(2,1)S(1)}, u32[]{:S(2)}, u32[]{:S(2)}) collective-permute-start(bf16[512,512]{1,0:T(8,128)(2,1)S(1)} %copy-done.16), channel_id=1, source_target_pairs={{0,8},{2,10},{12,4},{14,6},{1,9},{3,11},{13,5},{15,7},{16,24},{18,... | collective-permute-start | bytes 1572872 | tf_op jit(solution)/shard_map/over3/ppermute | solution.py:59
  119.9 8.2 %collective-permute-start.17 = (bf16[1024,512]{1,0:T(8,128)(2,1)S(1)}, bf16[1024,512]{1,0:T(8,128)(2,1)S(1)}, u32[]{:S(2)}, u32[]{:S(2)}) collective-permute-start(bf16[1024,512]{1,0:T(8,128)(2,1)S(1)} %pad_maximum_fusion.11), channel_id=1, source_target_pairs={{5,1},{7,3},{9,13},{11,15},{21,17},{23,19},{25,29},{27,31}} | collective-permute-start | bytes 3145736 | tf_op jit(solution)/shard_map/forward2/ppermute | solution.py:59
  121.4 11.4 %collective-permute-start.16 = (f32[512,512]{1,0:T(8,128)S(1)}, f32[512,512]{1,0:T(8,128)S(1)}, u32[]{:S(2)}, u32[]{:S(2)}) collective-permute-start(f32[512,512]{1,0:T(8,128)S(1)} %fusion.34), channel_id=1, source_target_pairs={{4,6},{6,4},{5,7},{7,5},{8,10},{10,8},{9,11},{11,9},{20,22},{22,20... | collective-permute-start | bytes 3145736 | tf_op jit(solution)/shard_map/c2/ppermute | solution.py:66
  128.1 3.0 %copy-start.23 = (bf16[1024,512]{1,0:T(8,128)(2,1)}, bf16[1024,512]{1,0:T(8,128)(2,1)S(1)}, u32[]{:S(2)}) copy-start(bf16[1024,512]{1,0:T(8,128)(2,1)S(1)} %collective-permute-done.17) | copy-start | bytes 3145732
  128.2 11.2 %collective-permute-start.23 = (bf16[1024,512]{1,0:T(8,128)(2,1)S(1)}, bf16[1024,512]{1,0:T(8,128)(2,1)S(1)}, u32[]{:S(2)}, u32[]{:S(2)}) collective-permute-start(bf16[1024,512]{1,0:T(8,128)(2,1)S(1)} %pad_maximum_fusion.12), channel_id=1, source_target_pairs={{5,1},{7,3},{9,13},{11,15},{21,17},{23,19},{25,29},{27,31}} | collective-permute-start | bytes 3145736 | tf_op jit(solution)/shard_map/forward3/ppermute | solution.py:59
  131.1 2.4 %copy-start.22 = (f32[512,1024]{1,0:T(8,128)}, f32[512,1024]{1,0:T(8,128)S(1)}, u32[]{:S(2)}) copy-start(f32[512,1024]{1,0:T(8,128)S(1)} %collective-permute-done.11) | copy-start | bytes 6291460
  131.1 11.8 %collective-permute-start.18 = (f32[512,512]{1,0:T(8,128)}, f32[512,512]{1,0:T(8,128)}, u32[]{:S(2)}, u32[]{:S(2)}) collective-permute-start(f32[512,512]{1,0:T(8,128)} %fusion.37), channel_id=1, source_target_pairs={{1,3},{3,1},{13,15},{15,13},{17,19},{19,17},{29,31},{31,29}} | collective-permute-start | bytes 3145736 | tf_op jit(solution)/shard_map/e2/ppermute | solution.py:66
  132.8 19.1 %collective-permute-start.22 = (f32[512,512]{1,0:T(8,128)S(1)}, f32[512,512]{1,0:T(8,128)S(1)}, u32[]{:S(2)}, u32[]{:S(2)}) collective-permute-start(f32[512,512]{1,0:T(8,128)S(1)} %fusion.33), channel_id=1, source_target_pairs={{4,6},{6,4},{5,7},{7,5},{8,10},{10,8},{9,11},{11,9},{20,22},{22,20... | collective-permute-start | bytes 3145736 | tf_op jit(solution)/shard_map/c3/ppermute | solution.py:66
  139.3 1.0 copy-start.25
  140.3 3.3 %copy-start.24 = (bf16[1024,512]{1,0:T(8,128)(2,1)S(1)}, bf16[1024,512]{1,0:T(8,128)(2,1)}, u32[]{:S(2)}) copy-start(bf16[1024,512]{1,0:T(8,128)(2,1)} %copy-done.23) | copy-start | bytes 3145732
  142.9 7.7 %collective-permute-start.24 = (f32[512,512]{1,0:T(8,128)S(1)}, f32[512,512]{1,0:T(8,128)S(1)}, u32[]{:S(2)}, u32[]{:S(2)}) collective-permute-start(f32[512,512]{1,0:T(8,128)S(1)} %fusion.36), channel_id=1, source_target_pairs={{1,3},{3,1},{13,15},{15,13},{17,19},{19,17},{29,31},{31,29}} | collective-permute-start | bytes 3145736 | tf_op jit(solution)/shard_map/e3/ppermute | solution.py:66
  147.7 2.9 %copy-start.26 = (bf16[1024,512]{1,0:T(8,128)(2,1)S(1)}, bf16[1024,512]{1,0:T(8,128)(2,1)}, u32[]{:S(2)}) copy-start(bf16[1024,512]{1,0:T(8,128)(2,1)} %copy-done.25) | copy-start | bytes 3145732
  147.8 25.0 %collective-permute-start.26 = (f32[128,1536]{1,0:T(8,128)S(1)}, f32[128,1536]{1,0:T(8,128)S(1)}, u32[]{:S(2)}, u32[]{:S(2)}) collective-permute-start(f32[128,1536]{1,0:T(8,128)S(1)} %slice.110), channel_id=1, source_target_pairs={{1,0},{3,2},{5,4},{7,6},{9,8},{11,10},{13,12},{15,14},{17,16},{19,... | collective-permute-start | bytes 2359304 | tf_op jit(solution)/shard_map/low_cross/ppermute | solution.py:245
  149.3 42.6 %collective-permute-start.19 = (f32[256,1536]{1,0:T(8,128)S(1)}, f32[256,1536]{1,0:T(8,128)S(1)}, u32[]{:S(2)}, u32[]{:S(2)}) collective-permute-start(f32[256,1536]{1,0:T(8,128)S(1)} %slice.102), channel_id=1, source_target_pairs={{4,0},{6,2},{8,12},{10,14},{20,16},{22,18},{24,28},{26,30}} | collective-permute-start | bytes 4718600 | tf_op jit(solution)/shard_map/end_diag/ppermute | solution.py:59
  153.2 29.9 %collective-permute-start.27 = (f32[128,512]{1,0:T(8,128)S(1)}, f32[128,512]{1,0:T(8,128)S(1)}, u32[]{:S(2)}, u32[]{:S(2)}) collective-permute-start(f32[128,512]{1,0:T(8,128)S(1)} %slice.113), channel_id=1, source_target_pairs={{1,0},{3,2},{5,4},{7,6},{9,8},{11,10},{13,12},{15,14},{17,16},{19,... | collective-permute-start | bytes 786440 | tf_op jit(solution)/shard_map/low_cross/ppermute | solution.py:245
  173.0 24.4 %collective-permute-start.25 = (f32[256,512]{1,0:T(8,128)S(1)}, f32[256,512]{1,0:T(8,128)S(1)}, u32[]{:S(2)}, u32[]{:S(2)}) collective-permute-start(f32[256,512]{1,0:T(8,128)S(1)} %slice.106), channel_id=1, source_target_pairs={{4,0},{6,2},{8,12},{10,14},{20,16},{22,18},{24,28},{26,30}} | collective-permute-start | bytes 1572872 | tf_op jit(solution)/shard_map/end_diag/ppermute | solution.py:59

commit v3 on v2

--- a/solution.py
+++ b/solution.py
@@ -113,7 +113,6 @@
     sent = [mine[2], mine[3], mine[0], mine[1]]
 
     a_moves = on_core(0, IN) + on_core(1, IN + OUT)
-    wide = [jnp.concatenate(mine[i : i + 2], 1) for i in (0, 2)]
     a, b, c = [None] * 4, [None] * 4, [None] * 4
 
     def gather(k, for_b=(), for_c=(), for_a=()):
@@ -124,10 +123,9 @@
             b[k] = permute(sb, BOTH(MID))
         with jax.named_scope(f"over{k}"):
             c[k] = permute(sc, BOTH(OVER))
-        if k % 2 == 0:
-            with jax.named_scope(f"half{k}"):
-                moved = permute(after(wide[k // 2], *for_a) if k else wide[0], a_moves)
-            a[k], a[k + 1] = moved[:, :group], moved[:, group:]
+        sa = mine[k] if k == 0 else after(mine[k], a[k - 1], *for_a)
+        with jax.named_scope(f"half{k}"):
+            a[k] = permute(sa, a_moves)
 
     def put(k):
         return jnp.concatenate([a[k], mine[k], b[k], c[k]], 0)
@@ -158,7 +156,7 @@
     gather(0)
     at_centre[0] = put(0)
     pu0 = part("cu0", cut(at_centre[0], 1 - x), at_centre[0])
-    gather(1, (), (pu0,))
+    gather(1, (), (pu0,), ())
     xu0 = swap("cu0", pu0, CENTRES)
     with jax.named_scope("across"):
         across = lax.ppermute(
@@ -168,20 +166,20 @@
             "feat",
             [(0, 1)],
         )
-    d[0] = forward(0)
+    d[0] = forward(0, pu0)
     at_centre[1] = put(1)
     centre_v = jnp.where(core == 0, at_centre[1], across)
     cl = lefts(at_centre[0], centre_v)
-    p1 = part("c1", cl[0], at_centre[1])
+    p1 = part("c1", cl[0], after(at_centre[1], c[1]))
     pv0 = part("cv0", cut(centre_v, 1 - x), at_centre[0])
     gather(2, (xu0,), (p1, pv0), (d[0],))
     x1 = swap("c1", after(p1, xu0), CENTRES)
-    xv0 = swap("cv0", pv0, CENTRES)
+    xv0 = swap("cv0", after(pv0, pv0), CENTRES)
     d[1] = forward(1, d[0])
     with jax.named_scope("given"):
         given = permute(after(at_centre[1][rows:], d[0]), [((cz, 0), (ez, 1)) for ez, cz in ENDS])
     at_centre[2] = put(2)
-    p2 = part("c2", cl[0], at_centre[2])
+    p2 = part("c2", cl[0], after(at_centre[2], c[2]))
 
     def at_end(k):
         return jnp.concatenate([mine[k], a[k], d[k]], 0)
@@ -189,9 +187,9 @@
     end_own = at_end(1)
     end_given = jnp.concatenate([across[:rows], given], 0)
     el = lefts(end_own, end_given)
-    near = jnp.concatenate([at_end(0), end_own], 1)
+    near = after(jnp.concatenate([at_end(0), end_own], 1), d[1])
     pe0 = part("e0", el[0], near)
-    gather(3, (xv0,), (p2, d[1]))
+    gather(3, (xv0,), (p2, d[1]), ())
     xe0 = swap("e0", pe0, ENDS_ONE)
 
     x2 = swap("c2", after(p2, x1, xv0), CENTRES)
@@ -231,32 +229,43 @@
         )
 
     with jax.named_scope("scores"):
-        other_scores = swap_core(after(partial_scores(1 - core), c[0]))
+        other_scores = swap_core(after(partial_scores(1 - core), x1))
     scores = (partial_scores(core) + other_scores).astype(jnp.bfloat16)
     scores = scores.reshape(2, row_count, half_targets)
 
-    def finish(ks):
-        result = jnp.concatenate(
-            [jnp.where(centre, by_centre[k], by_end[k]) for k in ks], 1
-        )
+    def send_diag(ks):
         with jax.named_scope("end_diag"):
-            end_diag = permute(result[block:], on_core(0, OUT))
+            return permute(jnp.concatenate([by_centre[k][block:] for k in ks], 1), on_core(0, OUT))
+
+    def send_cross(ks):
+        value = jnp.concatenate(
+            [
+                jnp.where(centre, by_centre[k], by_end[k])[block : block + block // 2]
+                for k in ks
+            ],
+            1,
+        )
         with jax.named_scope("low_cross"):
-            low_cross = lax.ppermute(result[block : block + block // 2], "feat", [(1, 0)])
-        diag = jnp.where((core == 0) & ~centre, end_diag, result[:block])
-        cross = jnp.where(core == 0, low_cross, result[block + block // 2 :])
-        return [
-            [v[:, i * group : (i + 1) * group] for i in range(len(ks))] for v in (diag, cross)
-        ]
-
-    first, last = finish((0, 1, 2)), finish((3,))
+            return lax.ppermute(value, "feat", [(1, 0)])
+
+    def split(values):
+        joined = jnp.concatenate(values, 1)
+        return [joined[:, i * group : (i + 1) * group] for i in range(4)]
+
+    end_diag = split([send_diag(ks) for ks in ((0, 1), (2,), (3,))])
+    low_cross = split([send_cross(ks) for ks in ((0, 1, 2), (3,))])
+    diag, cross = [], []
+    for k in range(4):
+        result = jnp.where(centre, by_centre[k], by_end[k])
+        diag.append(jnp.where((core == 0) & ~centre, end_diag[k], result[:block]))
+        cross.append(jnp.where(core == 0, low_cross[k], result[block + block // 2 :]))
 
     def assemble(p):
         p = [p[1], p[0], p[2], p[3]]
         return jnp.concatenate([jnp.where(lower, p[i], p[3 - i]) for i in range(4)], 1)
 
-    kernel_diag = assemble(first[0] + last[0])[None]
-    kernel_cross = assemble(first[1] + last[1])
+    kernel_diag = assemble(diag)[None]
+    kernel_cross = assemble(cross)
     return (kernel_diag, kernel_cross, scores)
 
 

time: 200 us -> 184 us (0.920)
  waiting for transfers between devices: 76.7 us -> 60.3 us
  starting transfers between devices: 54.2 us -> 65 us
  matrix products: 40.5 us -> 32.6 us
  local copies, waits for them, and re-layouts: 9.71 us -> 5.28 us
  other arithmetic: 16.5 us -> 18.7 us
    ppermute x2, waiting for transfers between devices: 27.2 us -> 0.01 us  [send_cross(): return lax.ppermute(value, 'feat', [(1, 0)])]
    ppermute x17 -> x20, starting transfers between devices: 42.2 us -> 53.9 us  [permute(): return lax.ppermute(value, ('ex', 'feat'), pairs)]
    ppermute x17 -> x20, waiting for transfers between devices: 49.5 us -> 60.3 us  [permute(): return lax.ppermute(value, ('ex', 'feat'), pairs)]
    concatenate x3, other arithmetic: 2.48 us -> 9.8 us  [the longest x1 9.67 us: gathering(): near = after(jnp.concatenate([at_end(0), end_own], 1), d[1])]
    dot_general x16, matrix products: 29.1 us -> 23.5 us  [gram_part(): lax.dot_general(left, right, (((0,), (0,)), ((), ())), preferred_element_...]
    unnamed x67 -> x29, local copies, waits for them, and re-layouts: 7.13 us -> 1.85 us
    slice x1 -> x0, other arithmetic: 2.69 us -> none  [gather(): a[k], a[k + 1] = (moved[:, :group], moved[:, group:])]
    dot_general x4, matrix products: 11.3 us -> 9.12 us  [partial_scores(): jnp.dot(s, t, preferred_element_type=jnp.float32)]
  transfers between devices with their start and end apart: 29 -> 32, of which waited for: 8 -> 6; matrix products, arithmetic and copies ran while one was open for 28% -> 28% of each run, Pallas kernels for 0% -> 0%
where the time goes in v3:
time: 184 us
  starting transfers between devices  65 us (35%)
  waiting for transfers between devices  60.3 us (33%)
  matrix products  32.6 us (18%)
  other arithmetic  18.7 us (10%)
  local copies, waits for them, and re-layouts  5.28 us (3%)
    ppermute x20, waiting for transfers between devices, permute(): return lax.ppermute(value, ('ex', 'feat'), pairs)  60.3 us
    ppermute x20, starting transfers between devices, permute(): return lax.ppermute(value, ('ex', 'feat'), pairs)  53.9 us
    dot_general x16, matrix products, gram_part(): lax.dot_general(left, right, (((0,), (0,)), ((), ())), preferred_element_...  23.5 us
    concatenate x1, other arithmetic, gathering(): near = after(jnp.concatenate([at_end(0), end_own], 1), d[1])  9.67 us
    dot_general x4, matrix products, partial_scores(): jnp.dot(s, t, preferred_element_type=jnp.float32)  9.12 us
    ppermute x8, starting transfers between devices, swap_x(): return lax.ppermute(value, ('ex', 'feat'), pairs)  6.97 us
  transfers between devices with their start and end apart: 32, of which 6 were waited for; matrix products, arithmetic and copies ran while one was open for 28% of the time, Pallas kernels for 0%

profile of v3, /device:TPU:0, one launch (start us, length us, event | category | flops | bytes accessed | tf_op | source)
XLA Modules:
  0.0 183.5 jit_solution(13029113884138969450)
XLA Ops:
  0.7 1.8 constant_dynamic-slice_fusion.10
  2.4 0.8 pad_maximum_fusion.31
  3.2 6.0 %collective-permute-start.4 = (bf16[512,512]{1,0:T(8,128)(2,1)}, bf16[512,512]{1,0:T(8,128)(2,1)S(1)}, u32[]{:S(2)}, u32[]{:S(2)}) collective-permute-start(bf16[512,512]{1,0:T(8,128)(2,1)} %pad_maximum_fusion.31), channel_id=1, source_target_pairs={{0,8},{2,10},{12,4},{14,6},{1,9},{3,11},{13,5},{15,7},{16,24},{18,... | collective-permute-start | bytes 1572872 | tf_op jit(solution)/shard_map/over0/ppermute | solution.py:59
  9.2 1.5 collective-permute-start.2
  10.7 0.9 pad_maximum_fusion.29
  11.5 2.3 %collective-permute-start = (bf16[512,512]{1,0:T(8,128)(2,1)}, bf16[512,512]{1,0:T(8,128)(2,1)S(1)}, u32[]{:S(2)}, u32[]{:S(2)}) collective-permute-start(bf16[512,512]{1,0:T(8,128)(2,1)} %pad_maximum_fusion.29), channel_id=1, source_target_pairs={{0,4},{2,6},{12,8},{14,10},{1,5},{3,7},{13,9},{15,11},{5,1},{7,3},... | collective-permute-start | bytes 1572872 | tf_op jit(solution)/shard_map/half0/ppermute | solution.py:59
  13.9 0.8 pad_maximum_fusion.30
  14.7 3.4 %fusion.23 = f32[256,512]{1,0:T(8,128)} fusion(bf16[256,2048]{1,0:T(8,128)(2,1)} %param.4, bf16[2048,1024]{1,0:T(8,128)(2,1)} %param.5, s32[]{:T(128)S(6)} %select_n.221), kind=kOutput, calls=%fused_computation.42 | convolution fusion | flops 536870912 | bytes 3670020 | tf_op jit(solution)/shard_map/scores/dot_general | solution.py:228
  18.1 2.7 %fusion.26 = f32[256,512]{1,0:T(8,128)S(1)} fusion(bf16[256,2048]{1,0:T(8,128)(2,1)} %param.3, bf16[2048,1024]{1,0:T(8,128)(2,1)} %param.5, s32[]{:T(128)S(6)} %select_n.221), kind=kOutput, calls=%fused_computation.43 | convolution fusion | flops 536870912 | bytes 3670020 | tf_op jit(solution)/shard_map/scores/dot_general | solution.py:228
  20.8 2.3 %fusion.17 = f32[256,512]{1,0:T(8,128)S(1)} fusion(bf16[256,2048]{1,0:T(8,128)(2,1)S(1)} %copy-done.1, bf16[2048,1024]{1,0:T(8,128)(2,1)} %param.5, s32[]{:T(128)S(6)} %select_n.220), kind=kOutput, calls=%fused_computation.40 | convolution fusion | flops 536870912 | bytes 3670020 | tf_op jit(solution)/shard_map/dot_general | solution.py:228
  23.1 8.8 %collective-permute-done = bf16[512,512]{1,0:T(8,128)(2,1)S(1)} collective-permute-done((bf16[512,512]{1,0:T(8,128)(2,1)}, bf16[512,512]{1,0:T(8,128)(2,1)S(1)}, u32[]{:S(2)}, u32[]{:S(2)}) %collective-permute-start) | collective-permute-done | bytes 524320 | tf_op jit(solution)/shard_map/half0/ppermute | solution.py:59
  32.2 4.3 %collective-permute-start.1 = (bf16[512,512]{1,0:T(8,128)(2,1)S(1)}, bf16[512,512]{1,0:T(8,128)(2,1)S(1)}, u32[]{:S(2)}, u32[]{:S(2)}) collective-permute-start(bf16[512,512]{1,0:T(8,128)(2,1)S(1)} %get-tuple-element.44), channel_id=1, source_target_pairs={{0,4},{2,6},{12,8},{14,10},{1,5},{3,7},{13,9},{15,11},{5,1},{7,3},... | collective-permute-start | bytes 1572872 | tf_op jit(solution)/shard_map/half1/ppermute | solution.py:59
  36.6 1.1 constant_dynamic-update-slice_fusion.11
  38.0 0.7 fusion.54
  39.0 0.8 collective-permute-start.3
  40.6 1.1 pad_maximum_fusion.10
  41.7 0.7 collective-permute-start.11
  42.5 1.4 collective-permute-start.6
  43.9 0.7 fusion.20
  44.7 11.2 %collective-permute-start.5 = (bf16[512,512]{1,0:T(8,128)(2,1)S(1)}, bf16[512,512]{1,0:T(8,128)(2,1)S(1)}, u32[]{:S(2)}, u32[]{:S(2)}) collective-permute-start(bf16[512,512]{1,0:T(8,128)(2,1)S(1)} %copy-done.3), channel_id=1, source_target_pairs={{0,8},{2,10},{12,4},{14,6},{1,9},{3,11},{13,5},{15,7},{16,24},{18,... | collective-permute-start | bytes 1572872 | tf_op jit(solution)/shard_map/over1/ppermute | solution.py:59
  56.7 1.5 fusion.15
  58.3 5.0 %collective-permute-start.15 = (bf16[512,512]{1,0:T(8,128)(2,1)}, bf16[512,512]{1,0:T(8,128)(2,1)S(1)}, u32[]{:S(2)}, u32[]{:S(2)}) collective-permute-start(bf16[512,512]{1,0:T(8,128)(2,1)} %pad_maximum_fusion.31), channel_id=1, source_target_pairs={{0,4},{2,6},{12,8},{14,10},{1,5},{3,7},{13,9},{15,11},{5,1},{7,3},... | collective-permute-start | bytes 1572872 | tf_op jit(solution)/shard_map/half2/ppermute | solution.py:59
  63.2 5.0 %collective-permute-done.5 = bf16[512,512]{1,0:T(8,128)(2,1)S(1)} collective-permute-done((bf16[512,512]{1,0:T(8,128)(2,1)S(1)}, bf16[512,512]{1,0:T(8,128)(2,1)S(1)}, u32[]{:S(2)}, u32[]{:S(2)}) %collective-permute-start.5) | collective-permute-done | bytes 524320 | tf_op jit(solution)/shard_map/over1/ppermute | solution.py:59
  68.5 0.7 collective-permute-start.12
  69.2 0.8 collective-permute-start.13
  70.0 7.4 %collective-permute-done.15 = bf16[512,512]{1,0:T(8,128)(2,1)S(1)} collective-permute-done((bf16[512,512]{1,0:T(8,128)(2,1)}, bf16[512,512]{1,0:T(8,128)(2,1)S(1)}, u32[]{:S(2)}, u32[]{:S(2)}) %collective-permute-start.15) | collective-permute-done | bytes 524320 | tf_op jit(solution)/shard_map/half2/ppermute | solution.py:59
  77.3 4.3 %collective-permute-start.16 = (bf16[512,512]{1,0:T(8,128)(2,1)S(1)}, bf16[512,512]{1,0:T(8,128)(2,1)S(1)}, u32[]{:S(2)}, u32[]{:S(2)}) collective-permute-start(bf16[512,512]{1,0:T(8,128)(2,1)S(1)} %copy-done.3), channel_id=1, source_target_pairs={{0,4},{2,6},{12,8},{14,10},{1,5},{3,7},{13,9},{15,11},{5,1},{7,3},... | collective-permute-start | bytes 1572872 | tf_op jit(solution)/shard_map/half3/ppermute | solution.py:59
  82.2 0.7 fusion.55
  83.6 2.2 %fusion.37 = f32[512,512]{1,0:T(8,128)} fusion(bf16[2048,512]{1,0:T(8,128)(2,1)S(1)} %constant_dynamic-update-slice_fusion.5, bf16[2048,256]{1,0:T(8,128)(2,1)S(1)} %get-tuple-element.70, bf16[2048,256]{1,0:T(8,128)(2,1)S(1)} %get-tuple-element.68), kind=kOutput, calls=%fused_computation.63 | convolution fusion | flops 1077936128 | bytes 5242880 | tf_op jit(solution)/shard_map/c1/dot_general | solution.py:10
  85.9 5.0 %collective-permute-start.19 = (bf16[512,512]{1,0:T(8,128)(2,1)}, bf16[512,512]{1,0:T(8,128)(2,1)S(1)}, u32[]{:S(2)}, u32[]{:S(2)}) collective-permute-start(bf16[512,512]{1,0:T(8,128)(2,1)} %pad_maximum_fusion.29), channel_id=1, source_target_pairs={{0,8},{2,10},{12,4},{14,6},{1,9},{3,11},{13,5},{15,7},{16,24},{18,... | collective-permute-start | bytes 1572872 | tf_op jit(solution)/shard_map/over2/ppermute | solution.py:59
  90.9 1.7 collective-permute-start.9
  92.6 9.7 %maximum_maximum_fusion = bf16[2048,1024]{1,0:T(8,128)(2,1)S(1)} fusion(bf16[1024,512]{1,0:T(8,128)(2,1)S(1)} %collective-permute-done.12, bf16[512,512]{1,0:T(8,128)(2,1)S(1)} %collective-permute-done.1, bf16[256,512]{1,0:T(8,128)(2,1)S(1)} %get-tuple-element.80, bf16[256,512]{1,0:T(8,128)(2,1)S(1)} %get-tuple-element.95, ...), kind=kLoop, calls=%fused_computation | loop fusion | flops 33554432 | bytes 8388608 | tf_op jit(solution)/shard_map/concatenate | solution.py:190
  102.7 0.9 slice-done
  103.7 2.3 %fusion.34 = f32[512,1024]{1,0:T(8,128)S(1)} fusion(bf16[2048,1024]{1,0:T(8,128)(2,1)S(1)} %maximum_maximum_fusion, bf16[2048,256]{1,0:T(8,128)(2,1)S(1)} %get-tuple-element.66, bf16[2048,256]{1,0:T(8,128)(2,1)S(1)} %get-tuple-element.64), kind=kOutput, calls=%fused_computation.60 | convolution fusion | flops 2151677952 | bytes 8388608 | tf_op jit(solution)/shard_map/e0/dot_general | solution.py:10
  106.0 0.8 collective-permute-start.14
  107.6 1.3 fusion.36
  108.9 4.7 %collective-permute-start.20 = (bf16[512,512]{1,0:T(8,128)(2,1)S(1)}, bf16[512,512]{1,0:T(8,128)(2,1)S(1)}, u32[]{:S(2)}, u32[]{:S(2)}) collective-permute-start(bf16[512,512]{1,0:T(8,128)(2,1)S(1)} %get-tuple-element.44), channel_id=1, source_target_pairs={{0,8},{2,10},{12,4},{14,6},{1,9},{3,11},{13,5},{15,7},{16,24},{18,... | collective-permute-start | bytes 1572872 | tf_op jit(solution)/shard_map/over3/ppermute | solution.py:59
  113.6 0.7 collective-permute-start.24
  114.4 0.7 fusion.16
  115.1 0.7 collective-permute-start.21
  115.9 7.9 %collective-permute-done.20 = bf16[512,512]{1,0:T(8,128)(2,1)S(1)} collective-permute-done((bf16[512,512]{1,0:T(8,128)(2,1)S(1)}, bf16[512,512]{1,0:T(8,128)(2,1)S(1)}, u32[]{:S(2)}, u32[]{:S(2)}) %collective-permute-start.20) | collective-permute-done | bytes 524320 | tf_op jit(solution)/shard_map/over3/ppermute | solution.py:59
  124.0 1.3 fusion.35
  125.3 0.7 collective-permute-start.25
  126.1 1.3 fusion.32
  127.4 0.7 collective-permute-start.22
  128.1 1.3 fusion.10
  129.4 1.3 collective-permute-start.28
  130.7 0.9 fusion.31
  131.7 0.9 collective-permute-start.26
  132.7 2.4 %add_multiply_fusion = f32[512,1024]{1,0:T(8,128)S(1)} fusion(f32[512,1024]{1,0:T(8,128)S(1)} %collective-permute-done.14, bf16[2048,1024]{1,0:T(8,128)(2,1)S(1)} %maximum_maximum_fusion, bf16[2048,256]{1,0:T(8,128)(2,1)S(1)} %get-tuple-element.65, bf16[2048,256]{1,0:T(8,128)(2,1)S(1)} %get-tuple-element.63), kind=kOutput, calls=%fused_computation.13 | convolution fusion | flops 2152726528 | bytes 10485760 | tf_op jit(solution)/shard_map/e0/dot_general | solution.py:10
  135.0 2.6 %slice_select_fusion = (f32[512,512]{1,0:T(8,128)S(1)}, f32[512,512]{1,0:T(8,128)S(1)}, f32[512,512]{1,0:T(8,128)S(1)}) fusion(f32[512,1024]{1,0:T(8,128)S(1)} %add_multiply_fusion, f32[256,512]{1,0:T(8,128)S(1)} %fusion.16, f32[256,512]{1,0:T(8,128)S(1)} %copy-done.6, pred[]{:T(512)S(6)} %or.3, f32[512,512]{1,0:T(8,128)} %collective-permute-done.9, ...), kind=kOutput, calls=%fused_computation.46 | convolution fusion | flops 1079246848 | bytes 11534337 | tf_op jit(solution)/shard_map/c1/dot_general | solution.py:10
  137.8 1.3 collective-permute-start.10
  139.2 1.3 fusion.33
  140.5 0.7 collective-permute-start.27
  141.2 1.3 fusion.13
  142.5 1.3 collective-permute-start.23
  143.8 1.3 fusion.9
  145.2 1.3 collective-permute-start.29
  146.5 1.3 fusion.12
  147.8 1.3 collective-permute-start.30
  149.1 9.8 %collective-permute-done.28 = f32[256,512]{1,0:T(8,128)S(1)} collective-permute-done((f32[256,512]{1,0:T(8,128)S(1)}, f32[256,512]{1,0:T(8,128)S(1)}, u32[]{:S(2)}, u32[]{:S(2)}) %collective-permute-start.28) | collective-permute-done | bytes 524320 | tf_op jit(solution)/shard_map/end_diag/ppermute | solution.py:59
  159.0 21.3 %collective-permute-done.23 = f32[256,512]{1,0:T(8,128)S(1)} collective-permute-done((f32[256,512]{1,0:T(8,128)S(1)}, f32[256,512]{1,0:T(8,128)S(1)}, u32[]{:S(2)}, u32[]{:S(2)}) %collective-permute-start.23) | collective-permute-done | bytes 524320 | tf_op jit(solution)/shard_map/end_diag/ppermute | solution.py:59
  180.8 1.5 maximum_bitcast_fusion
  182.5 1.0 pad_maximum_fusion.13
  (87 shorter events, 6.4 us)
Async XLA Ops:
  3.2 34.5 %collective-permute-start.4 = (bf16[512,512]{1,0:T(8,128)(2,1)}, bf16[512,512]{1,0:T(8,128)(2,1)S(1)}, u32[]{:S(2)}, u32[]{:S(2)}) collective-permute-start(bf16[512,512]{1,0:T(8,128)(2,1)} %pad_maximum_fusion.31), channel_id=1, source_target_pairs={{0,8},{2,10},{12,4},{14,6},{1,9},{3,11},{13,5},{15,7},{16,24},{18,... | collective-permute-start | bytes 1572872 | tf_op jit(solution)/shard_map/over0/ppermute | solution.py:59
  9.2 27.4 %collective-permute-start.2 = (bf16[512,512]{1,0:T(8,128)(2,1)}, bf16[512,512]{1,0:T(8,128)(2,1)}, u32[]{:S(2)}, u32[]{:S(2)}) collective-permute-start(bf16[512,512]{1,0:T(8,128)(2,1)} %pad_maximum_fusion.31), channel_id=1, source_target_pairs={{4,8},{6,10},{8,4},{10,6},{5,9},{7,11},{9,5},{11,7},{20,24},{22,26... | collective-permute-start | bytes 1572872 | tf_op jit(solution)/shard_map/middle0/ppermute | solution.py:59
  11.5 20.4 %collective-permute-start = (bf16[512,512]{1,0:T(8,128)(2,1)}, bf16[512,512]{1,0:T(8,128)(2,1)S(1)}, u32[]{:S(2)}, u32[]{:S(2)}) collective-permute-start(bf16[512,512]{1,0:T(8,128)(2,1)} %pad_maximum_fusion.29), channel_id=1, source_target_pairs={{0,4},{2,6},{12,8},{14,10},{1,5},{3,7},{13,9},{15,11},{5,1},{7,3},... | collective-permute-start | bytes 1572872 | tf_op jit(solution)/shard_map/half0/ppermute | solution.py:59
  18.1 2.7 %copy-start.1 = (bf16[256,2048]{1,0:T(8,128)(2,1)S(1)}, bf16[256,2048]{1,0:T(8,128)(2,1)}, u32[]{:S(2)}) copy-start(bf16[256,2048]{1,0:T(8,128)(2,1)} %param.4) | copy-start | bytes 3145732
  32.2 24.4 %collective-permute-start.1 = (bf16[512,512]{1,0:T(8,128)(2,1)S(1)}, bf16[512,512]{1,0:T(8,128)(2,1)S(1)}, u32[]{:S(2)}, u32[]{:S(2)}) collective-permute-start(bf16[512,512]{1,0:T(8,128)(2,1)S(1)} %get-tuple-element.44), channel_id=1, source_target_pairs={{0,4},{2,6},{12,8},{14,10},{1,5},{3,7},{13,9},{15,11},{5,1},{7,3},... | collective-permute-start | bytes 1572872 | tf_op jit(solution)/shard_map/half1/ppermute | solution.py:59
  38.0 1.0 copy-start.3
  38.0 2.6 %copy-start.4 = (f32[256,512]{1,0:T(8,128)S(1)}, f32[256,512]{1,0:T(8,128)}, u32[]{:S(2)}) copy-start(f32[256,512]{1,0:T(8,128)} %fusion.23) | copy-start | bytes 1572868
  38.0 5.9 %copy-start.5 = (bf16[2048,1024]{1,0:T(8,128)(2,1)S(1)}, bf16[2048,1024]{1,0:T(8,128)(2,1)}, u32[]{:S(2)}) copy-start(bf16[2048,1024]{1,0:T(8,128)(2,1)} %param.5) | copy-start | bytes 12582916
  39.0 4.9 %copy-start.2 = (bf16[256,2048]{1,0:T(8,128)(2,1)S(1)}, bf16[256,2048]{1,0:T(8,128)(2,1)}, u32[]{:S(2)}) copy-start(bf16[256,2048]{1,0:T(8,128)(2,1)} %param.3) | copy-start | bytes 3145732
  39.0 5.6 %collective-permute-start.3 = (bf16[512,512]{1,0:T(8,128)(2,1)S(1)}, bf16[512,512]{1,0:T(8,128)(2,1)S(1)}, u32[]{:S(2)}, u32[]{:S(2)}) collective-permute-start(bf16[512,512]{1,0:T(8,128)(2,1)S(1)} %copy-done.3), channel_id=1, source_target_pairs={{4,8},{6,10},{8,4},{10,6},{5,9},{7,11},{9,5},{11,7},{20,24},{22,26... | collective-permute-start | bytes 1572872 | tf_op jit(solution)/shard_map/middle1/ppermute | solution.py:59
  39.8 16.0 %collective-permute-start.8 = (f32[256,512]{1,0:T(8,128)S(1)}, f32[256,512]{1,0:T(8,128)S(1)}, u32[]{:S(2)}, u32[]{:S(2)}) collective-permute-start(f32[256,512]{1,0:T(8,128)S(1)} %fusion.54), channel_id=1, source_target_pairs={{4,6},{6,4},{5,7},{7,5},{8,10},{10,8},{9,11},{11,9},{20,22},{22,20... | collective-permute-start | bytes 1572872 | tf_op jit(solution)/shard_map/cu0/ppermute | solution.py:66
  41.7 16.5 %collective-permute-start.11 = (bf16[1024,512]{1,0:T(8,128)(2,1)S(1)}, bf16[1024,512]{1,0:T(8,128)(2,1)S(1)}, u32[]{:S(2)}, u32[]{:S(2)}) collective-permute-start(bf16[1024,512]{1,0:T(8,128)(2,1)S(1)} %pad_maximum_fusion.10), channel_id=1, source_target_pairs={{5,1},{7,3},{9,13},{11,15},{21,17},{23,19},{25,29},{27,31}} | collective-permute-start | bytes 3145736 | tf_op jit(solution)/shard_map/forward0/ppermute | solution.py:59
  42.5 39.3 %collective-permute-start.6 = (bf16[2048,512]{1,0:T(8,128)(2,1)S(1)}, bf16[2048,512]{1,0:T(8,128)(2,1)S(1)}, u32[]{:S(2)}, u32[]{:S(2)}) collective-permute-start(bf16[2048,512]{1,0:T(8,128)(2,1)S(1)} %get-tuple-element.83), channel_id=1, source_target_pairs={{0,1},{2,3},{4,5},{6,7},{8,9},{10,11},{12,13},{14,15},{16,17},{18,... | collective-permute-start | bytes 6291464 | tf_op jit(solution)/shard_map/across/ppermute | solution.py:162
  44.7 23.6 %collective-permute-start.5 = (bf16[512,512]{1,0:T(8,128)(2,1)S(1)}, bf16[512,512]{1,0:T(8,128)(2,1)S(1)}, u32[]{:S(2)}, u32[]{:S(2)}) collective-permute-start(bf16[512,512]{1,0:T(8,128)(2,1)S(1)} %copy-done.3), channel_id=1, source_target_pairs={{0,8},{2,10},{12,4},{14,6},{1,9},{3,11},{13,5},{15,7},{16,24},{18,... | collective-permute-start | bytes 1572872 | tf_op jit(solution)/shard_map/over1/ppermute | solution.py:59
  55.9 25.9 %collective-permute-start.17 = (bf16[512,512]{1,0:T(8,128)(2,1)}, bf16[512,512]{1,0:T(8,128)(2,1)S(1)}, u32[]{:S(2)}, u32[]{:S(2)}) collective-permute-start(bf16[512,512]{1,0:T(8,128)(2,1)} %pad_maximum_fusion.29), channel_id=1, source_target_pairs={{4,8},{6,10},{8,4},{10,6},{5,9},{7,11},{9,5},{11,7},{20,24},{22,26... | collective-permute-start | bytes 1572872 | tf_op jit(solution)/shard_map/middle2/ppermute | solution.py:59
  58.3 19.1 %collective-permute-start.15 = (bf16[512,512]{1,0:T(8,128)(2,1)}, bf16[512,512]{1,0:T(8,128)(2,1)S(1)}, u32[]{:S(2)}, u32[]{:S(2)}) collective-permute-start(bf16[512,512]{1,0:T(8,128)(2,1)} %pad_maximum_fusion.31), channel_id=1, source_target_pairs={{0,4},{2,6},{12,8},{14,10},{1,5},{3,7},{13,9},{15,11},{5,1},{7,3},... | collective-permute-start | bytes 1572872 | tf_op jit(solution)/shard_map/half2/ppermute | solution.py:59
  68.5 22.4 %collective-permute-start.12 = (bf16[1024,512]{1,0:T(8,128)(2,1)S(1)}, bf16[1024,512]{1,0:T(8,128)(2,1)S(1)}, u32[]{:S(2)}, u32[]{:S(2)}) collective-permute-start(bf16[1024,512]{1,0:T(8,128)(2,1)S(1)} %pad_maximum_fusion.9), channel_id=1, source_target_pairs={{5,1},{7,3},{9,13},{11,15},{21,17},{23,19},{25,29},{27,31}} | collective-permute-start | bytes 3145736 | tf_op jit(solution)/shard_map/forward1/ppermute | solution.py:59
  69.2 33.5 %collective-permute-start.13 = (bf16[1536,512]{1,0:T(8,128)(2,1)S(1)}, bf16[1536,512]{1,0:T(8,128)(2,1)S(1)}, u32[]{:S(2)}, u32[]{:S(2)}) collective-permute-start(bf16[1536,512]{1,0:T(8,128)(2,1)S(1)} %pad_maximum_fusion.7), channel_id=1, source_target_pairs={{4,1},{6,3},{8,13},{10,15},{20,17},{22,19},{24,29},{26,31}} | collective-permute-start | bytes 4718600 | tf_op jit(solution)/shard_map/given/ppermute | solution.py:59
  77.3 24.9 %collective-permute-start.16 = (bf16[512,512]{1,0:T(8,128)(2,1)S(1)}, bf16[512,512]{1,0:T(8,128)(2,1)S(1)}, u32[]{:S(2)}, u32[]{:S(2)}) collective-permute-start(bf16[512,512]{1,0:T(8,128)(2,1)S(1)} %copy-done.3), channel_id=1, source_target_pairs={{0,4},{2,6},{12,8},{14,10},{1,5},{3,7},{13,9},{15,11},{5,1},{7,3},... | collective-permute-start | bytes 1572872 | tf_op jit(solution)/shard_map/half3/ppermute | solution.py:59
  81.8 20.4 %copy-start = (bf16[2048,512]{1,0:T(8,128)(2,1)}, bf16[2048,512]{1,0:T(8,128)(2,1)S(1)}, u32[]{:S(2)}) copy-start(bf16[2048,512]{1,0:T(8,128)(2,1)S(1)} %collective-permute-done.6) | copy-start | bytes 6291460
  82.9 23.9 %collective-permute-start.7 = (f32[256,512]{1,0:T(8,128)S(1)}, f32[256,512]{1,0:T(8,128)S(1)}, u32[]{:S(2)}, u32[]{:S(2)}) collective-permute-start(f32[256,512]{1,0:T(8,128)S(1)} %fusion.55), channel_id=1, source_target_pairs={{4,6},{6,4},{5,7},{7,5},{8,10},{10,8},{9,11},{11,9},{20,22},{22,20... | collective-permute-start | bytes 1572872 | tf_op jit(solution)/shard_map/cv0/ppermute | solution.py:66
  85.9 21.7 %collective-permute-start.19 = (bf16[512,512]{1,0:T(8,128)(2,1)}, bf16[512,512]{1,0:T(8,128)(2,1)S(1)}, u32[]{:S(2)}, u32[]{:S(2)}) collective-permute-start(bf16[512,512]{1,0:T(8,128)(2,1)} %pad_maximum_fusion.29), channel_id=1, source_target_pairs={{0,8},{2,10},{12,4},{14,6},{1,9},{3,11},{13,5},{15,7},{16,24},{18,... | collective-permute-start | bytes 1572872 | tf_op jit(solution)/shard_map/over2/ppermute | solution.py:59
  90.9 24.2 %collective-permute-start.9 = (f32[512,512]{1,0:T(8,128)}, f32[512,512]{1,0:T(8,128)}, u32[]{:S(2)}, u32[]{:S(2)}) collective-permute-start(f32[512,512]{1,0:T(8,128)} %fusion.37), channel_id=1, source_target_pairs={{4,6},{6,4},{5,7},{7,5},{8,10},{10,8},{9,11},{11,9},{20,22},{22,20... | collective-permute-start | bytes 3145736 | tf_op jit(solution)/shard_map/c1/ppermute | solution.py:66
  102.5 1.0 slice-start
  106.0 25.7 %collective-permute-start.14 = (f32[512,1024]{1,0:T(8,128)S(1)}, f32[512,1024]{1,0:T(8,128)S(1)}, u32[]{:S(2)}, u32[]{:S(2)}) collective-permute-start(f32[512,1024]{1,0:T(8,128)S(1)} %fusion.34), channel_id=1, source_target_pairs={{1,3},{3,1},{13,15},{15,13},{17,19},{19,17},{29,31},{31,29}} | collective-permute-start | bytes 6291464 | tf_op jit(solution)/shard_map/e0/ppermute | solution.py:66
  106.9 9.0 %collective-permute-start.18 = (bf16[512,512]{1,0:T(8,128)(2,1)S(1)}, bf16[512,512]{1,0:T(8,128)(2,1)S(1)}, u32[]{:S(2)}, u32[]{:S(2)}) collective-permute-start(bf16[512,512]{1,0:T(8,128)(2,1)S(1)} %get-tuple-element.44), channel_id=1, source_target_pairs={{4,8},{6,10},{8,4},{10,6},{5,9},{7,11},{9,5},{11,7},{20,24},{22,26... | collective-permute-start | bytes 1572872 | tf_op jit(solution)/shard_map/middle3/ppermute | solution.py:59
  108.9 15.0 %collective-permute-start.20 = (bf16[512,512]{1,0:T(8,128)(2,1)S(1)}, bf16[512,512]{1,0:T(8,128)(2,1)S(1)}, u32[]{:S(2)}, u32[]{:S(2)}) collective-permute-start(bf16[512,512]{1,0:T(8,128)(2,1)S(1)} %get-tuple-element.44), channel_id=1, source_target_pairs={{0,8},{2,10},{12,4},{14,6},{1,9},{3,11},{13,5},{15,7},{16,24},{18,... | collective-permute-start | bytes 1572872 | tf_op jit(solution)/shard_map/over3/ppermute | solution.py:59
  113.6 11.7 %collective-permute-start.24 = (bf16[1024,512]{1,0:T(8,128)(2,1)S(1)}, bf16[1024,512]{1,0:T(8,128)(2,1)S(1)}, u32[]{:S(2)}, u32[]{:S(2)}) collective-permute-start(bf16[1024,512]{1,0:T(8,128)(2,1)S(1)} %pad_maximum_fusion.12), channel_id=1, source_target_pairs={{5,1},{7,3},{9,13},{11,15},{21,17},{23,19},{25,29},{27,31}} | collective-permute-start | bytes 3145736 | tf_op jit(solution)/shard_map/forward2/ppermute | solution.py:59
  115.1 12.2 %collective-permute-start.21 = (f32[512,512]{1,0:T(8,128)S(1)}, f32[512,512]{1,0:T(8,128)S(1)}, u32[]{:S(2)}, u32[]{:S(2)}) collective-permute-start(f32[512,512]{1,0:T(8,128)S(1)} %fusion.36), channel_id=1, source_target_pairs={{4,6},{6,4},{5,7},{7,5},{8,10},{10,8},{9,11},{11,9},{20,22},{22,20... | collective-permute-start | bytes 3145736 | tf_op jit(solution)/shard_map/c2/ppermute | solution.py:66
  123.9 6.8 %collective-permute-start.31 = (f32[512,512]{1,0:T(8,128)S(1)}, f32[512,512]{1,0:T(8,128)S(1)}, u32[]{:S(2)}, u32[]{:S(2)}) collective-permute-start(f32[512,512]{1,0:T(8,128)S(1)} %pad_maximum_fusion.14), channel_id=1, source_target_pairs={{0,1},{1,0},{2,3},{3,2},{4,5},{5,4},{6,7},{7,6},{8,9},{9,8},{10,11... | collective-permute-start | bytes 3145736 | tf_op jit(solution)/shard_map/scores/ppermute | solution.py:70
  125.3 13.8 %collective-permute-start.25 = (bf16[1024,512]{1,0:T(8,128)(2,1)S(1)}, bf16[1024,512]{1,0:T(8,128)(2,1)S(1)}, u32[]{:S(2)}, u32[]{:S(2)}) collective-permute-start(bf16[1024,512]{1,0:T(8,128)(2,1)S(1)} %pad_maximum_fusion.11), channel_id=1, source_target_pairs={{5,1},{7,3},{9,13},{11,15},{21,17},{23,19},{25,29},{27,31}} | collective-permute-start | bytes 3145736 | tf_op jit(solution)/shard_map/forward3/ppermute | solution.py:59
  127.4 13.8 %collective-permute-start.22 = (f32[512,512]{1,0:T(8,128)S(1)}, f32[512,512]{1,0:T(8,128)S(1)}, u32[]{:S(2)}, u32[]{:S(2)}) collective-permute-start(f32[512,512]{1,0:T(8,128)S(1)} %fusion.35), channel_id=1, source_target_pairs={{4,6},{6,4},{5,7},{7,5},{8,10},{10,8},{9,11},{11,9},{20,22},{22,20... | collective-permute-start | bytes 3145736 | tf_op jit(solution)/shard_map/c3/ppermute | solution.py:66
  129.4 29.5 %collective-permute-start.28 = (f32[256,512]{1,0:T(8,128)S(1)}, f32[256,512]{1,0:T(8,128)S(1)}, u32[]{:S(2)}, u32[]{:S(2)}) collective-permute-start(f32[256,512]{1,0:T(8,128)S(1)} %slice.114), channel_id=1, source_target_pairs={{4,0},{6,2},{8,12},{10,14},{20,16},{22,18},{24,28},{26,30}} | collective-permute-start | bytes 1572872 | tf_op jit(solution)/shard_map/end_diag/ppermute | solution.py:59
  131.7 8.8 %collective-permute-start.26 = (f32[512,512]{1,0:T(8,128)S(1)}, f32[512,512]{1,0:T(8,128)S(1)}, u32[]{:S(2)}, u32[]{:S(2)}) collective-permute-start(f32[512,512]{1,0:T(8,128)S(1)} %fusion.32), channel_id=1, source_target_pairs={{1,3},{3,1},{13,15},{15,13},{17,19},{19,17},{29,31},{31,29}} | collective-permute-start | bytes 3145736 | tf_op jit(solution)/shard_map/e2/ppermute | solution.py:66
  132.6 2.4 %copy-start.6 = (f32[256,512]{1,0:T(8,128)S(1)}, f32[256,512]{1,0:T(8,128)}, u32[]{:S(2)}) copy-start(f32[256,512]{1,0:T(8,128)} %fusion.15) | copy-start | bytes 1572868
  137.8 42.4 %collective-permute-start.10 = (f32[256,1024]{1,0:T(8,128)S(1)}, f32[256,1024]{1,0:T(8,128)S(1)}, u32[]{:S(2)}, u32[]{:S(2)}) collective-permute-start(f32[256,1024]{1,0:T(8,128)S(1)} %pad_maximum_fusion.8), channel_id=1, source_target_pairs={{4,0},{6,2},{8,12},{10,14},{20,16},{22,18},{24,28},{26,30}} | collective-permute-start | bytes 3145736 | tf_op jit(solution)/shard_map/end_diag/ppermute | solution.py:59
  140.5 6.0 %collective-permute-start.27 = (f32[512,512]{1,0:T(8,128)S(1)}, f32[512,512]{1,0:T(8,128)S(1)}, u32[]{:S(2)}, u32[]{:S(2)}) collective-permute-start(f32[512,512]{1,0:T(8,128)S(1)} %fusion.33), channel_id=1, source_target_pairs={{1,3},{3,1},{13,15},{15,13},{17,19},{19,17},{29,31},{31,29}} | collective-permute-start | bytes 3145736 | tf_op jit(solution)/shard_map/e3/ppermute | solution.py:66
  142.5 37.7 %collective-permute-start.23 = (f32[256,512]{1,0:T(8,128)S(1)}, f32[256,512]{1,0:T(8,128)S(1)}, u32[]{:S(2)}, u32[]{:S(2)}) collective-permute-start(f32[256,512]{1,0:T(8,128)S(1)} %slice.109), channel_id=1, source_target_pairs={{4,0},{6,2},{8,12},{10,14},{20,16},{22,18},{24,28},{26,30}} | collective-permute-start | bytes 1572872 | tf_op jit(solution)/shard_map/end_diag/ppermute | solution.py:59
  145.2 37.0 %collective-permute-start.29 = (f32[128,1536]{1,0:T(8,128)S(1)}, f32[128,1536]{1,0:T(8,128)S(1)}, u32[]{:S(2)}, u32[]{:S(2)}) collective-permute-start(f32[128,1536]{1,0:T(8,128)S(1)} %pad_maximum_fusion.15), channel_id=1, source_target_pairs={{1,0},{3,2},{5,4},{7,6},{9,8},{11,10},{13,12},{15,14},{17,16},{19,... | collective-permute-start | bytes 2359304 | tf_op jit(solution)/shard_map/low_cross/ppermute | solution.py:249
  147.8 34.4 %collective-permute-start.30 = (f32[128,512]{1,0:T(8,128)S(1)}, f32[128,512]{1,0:T(8,128)S(1)}, u32[]{:S(2)}, u32[]{:S(2)}) collective-permute-start(f32[128,512]{1,0:T(8,128)S(1)} %slice.121), channel_id=1, source_target_pairs={{1,0},{3,2},{5,4},{7,6},{9,8},{11,10},{13,12},{15,14},{17,16},{19,... | collective-permute-start | bytes 786440 | tf_op jit(solution)/shard_map/low_cross/ppermute | solution.py:249

commit v4 on v3

--- a/solution.py
+++ b/solution.py
@@ -156,7 +156,7 @@
     gather(0)
     at_centre[0] = put(0)
     pu0 = part("cu0", cut(at_centre[0], 1 - x), at_centre[0])
-    gather(1, (), (pu0,), ())
+    gather(1, (), (pu0,), (b[0],))
     xu0 = swap("cu0", pu0, CENTRES)
     with jax.named_scope("across"):
         across = lax.ppermute(
@@ -189,7 +189,7 @@
     el = lefts(end_own, end_given)
     near = after(jnp.concatenate([at_end(0), end_own], 1), d[1])
     pe0 = part("e0", el[0], near)
-    gather(3, (xv0,), (p2, d[1]), ())
+    gather(3, (xv0,), (p2,), ())
     xe0 = swap("e0", pe0, ENDS_ONE)
 
     x2 = swap("c2", after(p2, x1, xv0), CENTRES)
@@ -253,7 +253,7 @@
         return [joined[:, i * group : (i + 1) * group] for i in range(4)]
 
     end_diag = split([send_diag(ks) for ks in ((0, 1), (2,), (3,))])
-    low_cross = split([send_cross(ks) for ks in ((0, 1, 2), (3,))])
+    low_cross = split([send_cross(ks) for ks in ((0, 1), (2, 3))])
     diag, cross = [], []
     for k in range(4):
         result = jnp.where(centre, by_centre[k], by_end[k])

time: 184 us -> 183 us (level)
  no operation moved by 1% of the time
where the time goes in v4:
time: 183 us
  starting transfers between devices  65.3 us (36%)
  waiting for transfers between devices  59 us (32%)
  matrix products  32.6 us (18%)
  other arithmetic  18.7 us (10%)
  local copies, waits for them, and re-layouts  5.28 us (3%)
    ppermute x20, waiting for transfers between devices, permute(): return lax.ppermute(value, ('ex', 'feat'), pairs)  59 us
    ppermute x20, starting transfers between devices, permute(): return lax.ppermute(value, ('ex', 'feat'), pairs)  54.2 us
    dot_general x16, matrix products, gram_part(): lax.dot_general(left, right, (((0,), (0,)), ((), ())), preferred_element_...  23.5 us
    concatenate x1, other arithmetic, gathering(): near = after(jnp.concatenate([at_end(0), end_own], 1), d[1])  9.67 us
    dot_general x4, matrix products, partial_scores(): jnp.dot(s, t, preferred_element_type=jnp.float32)  9.12 us
    ppermute x8, starting transfers between devices, swap_x(): return lax.ppermute(value, ('ex', 'feat'), pairs)  6.97 us
  transfers between devices with their start and end apart: 32, of which 6 were waited for; matrix products, arithmetic and copies ran while one was open for 28% of the time, Pallas kernels for 0%

profile of v4, /device:TPU:0, one launch (start us, length us, event | category | flops | bytes accessed | tf_op | source)
XLA Modules:
  0.0 182.6 jit_solution(4166706670621136149)
XLA Ops:
  0.7 1.8 constant_dynamic-slice_fusion.10
  2.4 0.8 pad_maximum_fusion.29
  3.9 8.4 %collective-permute-start.4 = (bf16[512,512]{1,0:T(8,128)(2,1)}, bf16[512,512]{1,0:T(8,128)(2,1)}, u32[]{:S(2)}, u32[]{:S(2)}) collective-permute-start(bf16[512,512]{1,0:T(8,128)(2,1)} %pad_maximum_fusion.29), channel_id=1, source_target_pairs={{0,8},{2,10},{12,4},{14,6},{1,9},{3,11},{13,5},{15,7},{16,24},{18,... | collective-permute-start | bytes 1572872 | tf_op jit(solution)/shard_map/over0/ppermute | solution.py:59
  12.3 0.9 pad_maximum_fusion.28
  13.2 1.3 collective-permute-start
  14.5 0.8 pad_maximum_fusion.30
  15.4 3.4 %fusion.23 = f32[256,512]{1,0:T(8,128)} fusion(bf16[256,2048]{1,0:T(8,128)(2,1)} %param.4, bf16[2048,1024]{1,0:T(8,128)(2,1)} %param.5, s32[]{:T(128)S(6)} %select_n.221), kind=kOutput, calls=%fused_computation.42 | convolution fusion | flops 536870912 | bytes 3670020 | tf_op jit(solution)/shard_map/scores/dot_general | solution.py:228
  18.8 2.7 %fusion.26 = f32[256,512]{1,0:T(8,128)S(1)} fusion(bf16[256,2048]{1,0:T(8,128)(2,1)} %param.3, bf16[2048,1024]{1,0:T(8,128)(2,1)} %param.5, s32[]{:T(128)S(6)} %select_n.221), kind=kOutput, calls=%fused_computation.43 | convolution fusion | flops 536870912 | bytes 3670020 | tf_op jit(solution)/shard_map/scores/dot_general | solution.py:228
  21.5 2.3 %fusion.17 = f32[256,512]{1,0:T(8,128)S(1)} fusion(bf16[256,2048]{1,0:T(8,128)(2,1)S(1)} %copy-done.1, bf16[2048,1024]{1,0:T(8,128)(2,1)} %param.5, s32[]{:T(128)S(6)} %select_n.220), kind=kOutput, calls=%fused_computation.40 | convolution fusion | flops 536870912 | bytes 3670020 | tf_op jit(solution)/shard_map/dot_general | solution.py:228
  23.8 10.2 %collective-permute-done = bf16[512,512]{1,0:T(8,128)(2,1)S(1)} collective-permute-done((bf16[512,512]{1,0:T(8,128)(2,1)}, bf16[512,512]{1,0:T(8,128)(2,1)S(1)}, u32[]{:S(2)}, u32[]{:S(2)}) %collective-permute-start) | collective-permute-done | bytes 524320 | tf_op jit(solution)/shard_map/half0/ppermute | solution.py:59
  34.3 4.3 %collective-permute-start.2 = (bf16[512,512]{1,0:T(8,128)(2,1)S(1)}, bf16[512,512]{1,0:T(8,128)(2,1)S(1)}, u32[]{:S(2)}, u32[]{:S(2)}) collective-permute-start(bf16[512,512]{1,0:T(8,128)(2,1)S(1)} %get-tuple-element.44), channel_id=1, source_target_pairs={{0,4},{2,6},{12,8},{14,10},{1,5},{3,7},{13,9},{15,11},{5,1},{7,3},... | collective-permute-start | bytes 1572872 | tf_op jit(solution)/shard_map/half1/ppermute | solution.py:59
  38.8 1.1 constant_dynamic-update-slice_fusion.10
  40.1 0.7 fusion.54
  41.1 0.8 collective-permute-start.3
  41.9 0.7 collective-permute-start.8
  42.7 1.1 pad_maximum_fusion.10
  43.8 0.7 collective-permute-start.11
  44.6 1.4 collective-permute-start.6
  46.0 0.7 fusion.20
  46.8 11.9 %collective-permute-start.5 = (bf16[512,512]{1,0:T(8,128)(2,1)S(1)}, bf16[512,512]{1,0:T(8,128)(2,1)S(1)}, u32[]{:S(2)}, u32[]{:S(2)}) collective-permute-start(bf16[512,512]{1,0:T(8,128)(2,1)S(1)} %copy-done.3), channel_id=1, source_target_pairs={{0,8},{2,10},{12,4},{14,6},{1,9},{3,11},{13,5},{15,7},{16,24},{18,... | collective-permute-start | bytes 1572872 | tf_op jit(solution)/shard_map/over1/ppermute | solution.py:59
  59.6 1.5 fusion.15
  61.1 3.8 %collective-permute-start.15 = (bf16[512,512]{1,0:T(8,128)(2,1)}, bf16[512,512]{1,0:T(8,128)(2,1)S(1)}, u32[]{:S(2)}, u32[]{:S(2)}) collective-permute-start(bf16[512,512]{1,0:T(8,128)(2,1)} %pad_maximum_fusion.29), channel_id=1, source_target_pairs={{0,4},{2,6},{12,8},{14,10},{1,5},{3,7},{13,9},{15,11},{5,1},{7,3},... | collective-permute-start | bytes 1572872 | tf_op jit(solution)/shard_map/half2/ppermute | solution.py:59
  64.9 6.1 %collective-permute-done.5 = bf16[512,512]{1,0:T(8,128)(2,1)S(1)} collective-permute-done((bf16[512,512]{1,0:T(8,128)(2,1)S(1)}, bf16[512,512]{1,0:T(8,128)(2,1)S(1)}, u32[]{:S(2)}, u32[]{:S(2)}) %collective-permute-start.5) | collective-permute-done | bytes 524320 | tf_op jit(solution)/shard_map/over1/ppermute | solution.py:59
  71.3 0.7 collective-permute-start.12
  72.0 0.8 collective-permute-start.13
  72.8 7.0 %collective-permute-done.15 = bf16[512,512]{1,0:T(8,128)(2,1)S(1)} collective-permute-done((bf16[512,512]{1,0:T(8,128)(2,1)}, bf16[512,512]{1,0:T(8,128)(2,1)S(1)}, u32[]{:S(2)}, u32[]{:S(2)}) %collective-permute-start.15) | collective-permute-done | bytes 524320 | tf_op jit(solution)/shard_map/half2/ppermute | solution.py:59
  79.8 4.3 %collective-permute-start.16 = (bf16[512,512]{1,0:T(8,128)(2,1)S(1)}, bf16[512,512]{1,0:T(8,128)(2,1)S(1)}, u32[]{:S(2)}, u32[]{:S(2)}) collective-permute-start(bf16[512,512]{1,0:T(8,128)(2,1)S(1)} %copy-done.3), channel_id=1, source_target_pairs={{0,4},{2,6},{12,8},{14,10},{1,5},{3,7},{13,9},{15,11},{5,1},{7,3},... | collective-permute-start | bytes 1572872 | tf_op jit(solution)/shard_map/half3/ppermute | solution.py:59
  84.6 0.7 fusion.55
  86.1 2.2 %fusion.37 = f32[512,512]{1,0:T(8,128)} fusion(bf16[2048,512]{1,0:T(8,128)(2,1)S(1)} %constant_dynamic-update-slice_fusion.5, bf16[2048,256]{1,0:T(8,128)(2,1)S(1)} %get-tuple-element.70, bf16[2048,256]{1,0:T(8,128)(2,1)S(1)} %get-tuple-element.68), kind=kOutput, calls=%fused_computation.62 | convolution fusion | flops 1077936128 | bytes 5242880 | tf_op jit(solution)/shard_map/c1/dot_general | solution.py:10
  88.3 3.9 %collective-permute-start.19 = (bf16[512,512]{1,0:T(8,128)(2,1)}, bf16[512,512]{1,0:T(8,128)(2,1)S(1)}, u32[]{:S(2)}, u32[]{:S(2)}) collective-permute-start(bf16[512,512]{1,0:T(8,128)(2,1)} %pad_maximum_fusion.28), channel_id=1, source_target_pairs={{0,8},{2,10},{12,4},{14,6},{1,9},{3,11},{13,5},{15,7},{16,24},{18,... | collective-permute-start | bytes 1572872 | tf_op jit(solution)/shard_map/over2/ppermute | solution.py:59
  92.2 1.7 collective-permute-start.9
  93.9 9.7 %maximum_maximum_fusion = bf16[2048,1024]{1,0:T(8,128)(2,1)S(1)} fusion(bf16[1024,512]{1,0:T(8,128)(2,1)S(1)} %collective-permute-done.12, bf16[512,512]{1,0:T(8,128)(2,1)S(1)} %collective-permute-done.2, bf16[256,512]{1,0:T(8,128)(2,1)S(1)} %get-tuple-element.82, bf16[256,512]{1,0:T(8,128)(2,1)S(1)} %get-tuple-element.95, ...), kind=kLoop, calls=%fused_computation | loop fusion | flops 33554432 | bytes 8388608 | tf_op jit(solution)/shard_map/concatenate | solution.py:190
  104.0 0.9 slice-done
  105.0 2.3 %fusion.34 = f32[512,1024]{1,0:T(8,128)S(1)} fusion(bf16[2048,1024]{1,0:T(8,128)(2,1)S(1)} %maximum_maximum_fusion, bf16[2048,256]{1,0:T(8,128)(2,1)S(1)} %get-tuple-element.66, bf16[2048,256]{1,0:T(8,128)(2,1)S(1)} %get-tuple-element.64), kind=kOutput, calls=%fused_computation.59 | convolution fusion | flops 2151677952 | bytes 8388608 | tf_op jit(solution)/shard_map/e0/dot_general | solution.py:10
  107.3 0.8 collective-permute-start.14
  108.9 1.3 fusion.36
  110.2 5.8 %collective-permute-start.20 = (bf16[512,512]{1,0:T(8,128)(2,1)S(1)}, bf16[512,512]{1,0:T(8,128)(2,1)S(1)}, u32[]{:S(2)}, u32[]{:S(2)}) collective-permute-start(bf16[512,512]{1,0:T(8,128)(2,1)S(1)} %get-tuple-element.44), channel_id=1, source_target_pairs={{0,8},{2,10},{12,4},{14,6},{1,9},{3,11},{13,5},{15,7},{16,24},{18,... | collective-permute-start | bytes 1572872 | tf_op jit(solution)/shard_map/over3/ppermute | solution.py:59
  116.1 0.7 collective-permute-start.24
  116.8 0.7 fusion.16
  117.6 0.7 collective-permute-start.21
  118.3 6.6 %collective-permute-done.20 = bf16[512,512]{1,0:T(8,128)(2,1)S(1)} collective-permute-done((bf16[512,512]{1,0:T(8,128)(2,1)S(1)}, bf16[512,512]{1,0:T(8,128)(2,1)S(1)}, u32[]{:S(2)}, u32[]{:S(2)}) %collective-permute-start.20) | collective-permute-done | bytes 524320 | tf_op jit(solution)/shard_map/over3/ppermute | solution.py:59
  125.1 1.3 fusion.35
  126.4 0.7 collective-permute-start.25
  127.2 1.3 fusion.32
  128.5 0.7 collective-permute-start.22
  129.2 1.3 fusion.10
  130.5 1.3 collective-permute-start.28
  131.8 0.9 fusion.31
  132.8 0.9 collective-permute-start.26
  133.7 2.4 %add_multiply_fusion = f32[512,1024]{1,0:T(8,128)S(1)} fusion(f32[512,1024]{1,0:T(8,128)S(1)} %collective-permute-done.14, bf16[2048,1024]{1,0:T(8,128)(2,1)S(1)} %maximum_maximum_fusion, bf16[2048,256]{1,0:T(8,128)(2,1)S(1)} %get-tuple-element.65, bf16[2048,256]{1,0:T(8,128)(2,1)S(1)} %get-tuple-element.63), kind=kOutput, calls=%fused_computation.13 | convolution fusion | flops 2152726528 | bytes 10485760 | tf_op jit(solution)/shard_map/e0/dot_general | solution.py:10
  136.1 2.7 %slice_select_fusion = (f32[512,512]{1,0:T(8,128)S(1)}, f32[512,512]{1,0:T(8,128)S(1)}, f32[512,512]{1,0:T(8,128)S(1)}) fusion(f32[512,1024]{1,0:T(8,128)S(1)} %add_multiply_fusion, f32[256,512]{1,0:T(8,128)S(1)} %fusion.16, f32[256,512]{1,0:T(8,128)S(1)} %copy-done.6, pred[]{:T(512)S(6)} %or.3, f32[512,512]{1,0:T(8,128)} %collective-permute-done.9, ...), kind=kOutput, calls=%fused_computation.46 | convolution fusion | flops 1079246848 | bytes 11534337 | tf_op jit(solution)/shard_map/c1/dot_general | solution.py:10
  138.9 1.3 collective-permute-start.10
  140.3 1.3 fusion.33
  141.6 0.7 collective-permute-start.27
  142.3 1.3 collective-permute-start.29
  143.7 1.3 fusion.13
  145.0 1.3 collective-permute-start.23
  146.3 1.3 fusion.9
  147.6 1.3 fusion.12
  149.0 1.3 collective-permute-start.30
  150.3 8.8 %collective-permute-done.28 = f32[256,512]{1,0:T(8,128)S(1)} collective-permute-done((f32[256,512]{1,0:T(8,128)S(1)}, f32[256,512]{1,0:T(8,128)S(1)}, u32[]{:S(2)}, u32[]{:S(2)}) %collective-permute-start.28) | collective-permute-done | bytes 524320 | tf_op jit(solution)/shard_map/end_diag/ppermute | solution.py:59
  159.1 20.2 %collective-permute-done.23 = f32[256,512]{1,0:T(8,128)S(1)} collective-permute-done((f32[256,512]{1,0:T(8,128)S(1)}, f32[256,512]{1,0:T(8,128)S(1)}, u32[]{:S(2)}, u32[]{:S(2)}) %collective-permute-start.23) | collective-permute-done | bytes 524320 | tf_op jit(solution)/shard_map/end_diag/ppermute | solution.py:59
  179.8 1.5 maximum_bitcast_fusion
  181.5 1.0 pad_maximum_fusion.13
  (88 shorter events, 6.4 us)
Async XLA Ops:
  3.2 31.0 %collective-permute-start.1 = (bf16[512,512]{1,0:T(8,128)(2,1)}, bf16[512,512]{1,0:T(8,128)(2,1)S(1)}, u32[]{:S(2)}, u32[]{:S(2)}) collective-permute-start(bf16[512,512]{1,0:T(8,128)(2,1)} %pad_maximum_fusion.29), channel_id=1, source_target_pairs={{4,8},{6,10},{8,4},{10,6},{5,9},{7,11},{9,5},{11,7},{20,24},{22,26... | collective-permute-start | bytes 1572872 | tf_op jit(solution)/shard_map/middle0/ppermute | solution.py:59
  3.9 34.8 %collective-permute-start.4 = (bf16[512,512]{1,0:T(8,128)(2,1)}, bf16[512,512]{1,0:T(8,128)(2,1)}, u32[]{:S(2)}, u32[]{:S(2)}) collective-permute-start(bf16[512,512]{1,0:T(8,128)(2,1)} %pad_maximum_fusion.29), channel_id=1, source_target_pairs={{0,8},{2,10},{12,4},{14,6},{1,9},{3,11},{13,5},{15,7},{16,24},{18,... | collective-permute-start | bytes 1572872 | tf_op jit(solution)/shard_map/over0/ppermute | solution.py:59
  13.2 20.8 %collective-permute-start = (bf16[512,512]{1,0:T(8,128)(2,1)}, bf16[512,512]{1,0:T(8,128)(2,1)S(1)}, u32[]{:S(2)}, u32[]{:S(2)}) collective-permute-start(bf16[512,512]{1,0:T(8,128)(2,1)} %pad_maximum_fusion.28), channel_id=1, source_target_pairs={{0,4},{2,6},{12,8},{14,10},{1,5},{3,7},{13,9},{15,11},{5,1},{7,3},... | collective-permute-start | bytes 1572872 | tf_op jit(solution)/shard_map/half0/ppermute | solution.py:59
  18.8 2.7 %copy-start.1 = (bf16[256,2048]{1,0:T(8,128)(2,1)S(1)}, bf16[256,2048]{1,0:T(8,128)(2,1)}, u32[]{:S(2)}) copy-start(bf16[256,2048]{1,0:T(8,128)(2,1)} %param.4) | copy-start | bytes 3145732
  34.3 25.1 %collective-permute-start.2 = (bf16[512,512]{1,0:T(8,128)(2,1)S(1)}, bf16[512,512]{1,0:T(8,128)(2,1)S(1)}, u32[]{:S(2)}, u32[]{:S(2)}) collective-permute-start(bf16[512,512]{1,0:T(8,128)(2,1)S(1)} %get-tuple-element.44), channel_id=1, source_target_pairs={{0,4},{2,6},{12,8},{14,10},{1,5},{3,7},{13,9},{15,11},{5,1},{7,3},... | collective-permute-start | bytes 1572872 | tf_op jit(solution)/shard_map/half1/ppermute | solution.py:59
  40.1 1.0 copy-start.3
  40.1 2.6 %copy-start.4 = (f32[256,512]{1,0:T(8,128)S(1)}, f32[256,512]{1,0:T(8,128)}, u32[]{:S(2)}) copy-start(f32[256,512]{1,0:T(8,128)} %fusion.23) | copy-start | bytes 1572868
  40.1 5.9 %copy-start.5 = (bf16[2048,1024]{1,0:T(8,128)(2,1)S(1)}, bf16[2048,1024]{1,0:T(8,128)(2,1)}, u32[]{:S(2)}) copy-start(bf16[2048,1024]{1,0:T(8,128)(2,1)} %param.5) | copy-start | bytes 12582916
  41.1 4.9 %copy-start.2 = (bf16[256,2048]{1,0:T(8,128)(2,1)S(1)}, bf16[256,2048]{1,0:T(8,128)(2,1)}, u32[]{:S(2)}) copy-start(bf16[256,2048]{1,0:T(8,128)(2,1)} %param.3) | copy-start | bytes 3145732
  41.1 5.6 %collective-permute-start.3 = (bf16[512,512]{1,0:T(8,128)(2,1)S(1)}, bf16[512,512]{1,0:T(8,128)(2,1)S(1)}, u32[]{:S(2)}, u32[]{:S(2)}) collective-permute-start(bf16[512,512]{1,0:T(8,128)(2,1)S(1)} %copy-done.3), channel_id=1, source_target_pairs={{4,8},{6,10},{8,4},{10,6},{5,9},{7,11},{9,5},{11,7},{20,24},{22,26... | collective-permute-start | bytes 1572872 | tf_op jit(solution)/shard_map/middle1/ppermute | solution.py:59
  41.9 16.8 %collective-permute-start.8 = (f32[256,512]{1,0:T(8,128)S(1)}, f32[256,512]{1,0:T(8,128)S(1)}, u32[]{:S(2)}, u32[]{:S(2)}) collective-permute-start(f32[256,512]{1,0:T(8,128)S(1)} %fusion.54), channel_id=1, source_target_pairs={{4,6},{6,4},{5,7},{7,5},{8,10},{10,8},{9,11},{11,9},{20,22},{22,20... | collective-permute-start | bytes 1572872 | tf_op jit(solution)/shard_map/cu0/ppermute | solution.py:66
  43.8 17.3 %collective-permute-start.11 = (bf16[1024,512]{1,0:T(8,128)(2,1)S(1)}, bf16[1024,512]{1,0:T(8,128)(2,1)S(1)}, u32[]{:S(2)}, u32[]{:S(2)}) collective-permute-start(bf16[1024,512]{1,0:T(8,128)(2,1)S(1)} %pad_maximum_fusion.10), channel_id=1, source_target_pairs={{5,1},{7,3},{9,13},{11,15},{21,17},{23,19},{25,29},{27,31}} | collective-permute-start | bytes 3145736 | tf_op jit(solution)/shard_map/forward0/ppermute | solution.py:59
  44.6 39.7 %collective-permute-start.6 = (bf16[2048,512]{1,0:T(8,128)(2,1)S(1)}, bf16[2048,512]{1,0:T(8,128)(2,1)S(1)}, u32[]{:S(2)}, u32[]{:S(2)}) collective-permute-start(bf16[2048,512]{1,0:T(8,128)(2,1)S(1)} %get-tuple-element.83), channel_id=1, source_target_pairs={{0,1},{2,3},{4,5},{6,7},{8,9},{10,11},{12,13},{14,15},{16,17},{18,... | collective-permute-start | bytes 6291464 | tf_op jit(solution)/shard_map/across/ppermute | solution.py:162
  46.8 24.3 %collective-permute-start.5 = (bf16[512,512]{1,0:T(8,128)(2,1)S(1)}, bf16[512,512]{1,0:T(8,128)(2,1)S(1)}, u32[]{:S(2)}, u32[]{:S(2)}) collective-permute-start(bf16[512,512]{1,0:T(8,128)(2,1)S(1)} %copy-done.3), channel_id=1, source_target_pairs={{0,8},{2,10},{12,4},{14,6},{1,9},{3,11},{13,5},{15,7},{16,24},{18,... | collective-permute-start | bytes 1572872 | tf_op jit(solution)/shard_map/over1/ppermute | solution.py:59
  58.7 25.5 %collective-permute-start.17 = (bf16[512,512]{1,0:T(8,128)(2,1)}, bf16[512,512]{1,0:T(8,128)(2,1)S(1)}, u32[]{:S(2)}, u32[]{:S(2)}) collective-permute-start(bf16[512,512]{1,0:T(8,128)(2,1)} %pad_maximum_fusion.28), channel_id=1, source_target_pairs={{4,8},{6,10},{8,4},{10,6},{5,9},{7,11},{9,5},{11,7},{20,24},{22,26... | collective-permute-start | bytes 1572872 | tf_op jit(solution)/shard_map/middle2/ppermute | solution.py:59
  61.1 18.7 %collective-permute-start.15 = (bf16[512,512]{1,0:T(8,128)(2,1)}, bf16[512,512]{1,0:T(8,128)(2,1)S(1)}, u32[]{:S(2)}, u32[]{:S(2)}) collective-permute-start(bf16[512,512]{1,0:T(8,128)(2,1)} %pad_maximum_fusion.29), channel_id=1, source_target_pairs={{0,4},{2,6},{12,8},{14,10},{1,5},{3,7},{13,9},{15,11},{5,1},{7,3},... | collective-permute-start | bytes 1572872 | tf_op jit(solution)/shard_map/half2/ppermute | solution.py:59
  71.3 20.9 %collective-permute-start.12 = (bf16[1024,512]{1,0:T(8,128)(2,1)S(1)}, bf16[1024,512]{1,0:T(8,128)(2,1)S(1)}, u32[]{:S(2)}, u32[]{:S(2)}) collective-permute-start(bf16[1024,512]{1,0:T(8,128)(2,1)S(1)} %pad_maximum_fusion.9), channel_id=1, source_target_pairs={{5,1},{7,3},{9,13},{11,15},{21,17},{23,19},{25,29},{27,31}} | collective-permute-start | bytes 3145736 | tf_op jit(solution)/shard_map/forward1/ppermute | solution.py:59
  72.0 31.9 %collective-permute-start.13 = (bf16[1536,512]{1,0:T(8,128)(2,1)S(1)}, bf16[1536,512]{1,0:T(8,128)(2,1)S(1)}, u32[]{:S(2)}, u32[]{:S(2)}) collective-permute-start(bf16[1536,512]{1,0:T(8,128)(2,1)S(1)} %pad_maximum_fusion.7), channel_id=1, source_target_pairs={{4,1},{6,3},{8,13},{10,15},{20,17},{22,19},{24,29},{26,31}} | collective-permute-start | bytes 4718600 | tf_op jit(solution)/shard_map/given/ppermute | solution.py:59
  79.8 23.8 %collective-permute-start.16 = (bf16[512,512]{1,0:T(8,128)(2,1)S(1)}, bf16[512,512]{1,0:T(8,128)(2,1)S(1)}, u32[]{:S(2)}, u32[]{:S(2)}) collective-permute-start(bf16[512,512]{1,0:T(8,128)(2,1)S(1)} %copy-done.3), channel_id=1, source_target_pairs={{0,4},{2,6},{12,8},{14,10},{1,5},{3,7},{13,9},{15,11},{5,1},{7,3},... | collective-permute-start | bytes 1572872 | tf_op jit(solution)/shard_map/half3/ppermute | solution.py:59
  84.2 19.3 %copy-start = (bf16[2048,512]{1,0:T(8,128)(2,1)}, bf16[2048,512]{1,0:T(8,128)(2,1)S(1)}, u32[]{:S(2)}) copy-start(bf16[2048,512]{1,0:T(8,128)(2,1)S(1)} %collective-permute-done.6) | copy-start | bytes 6291460
  85.4 22.8 %collective-permute-start.7 = (f32[256,512]{1,0:T(8,128)S(1)}, f32[256,512]{1,0:T(8,128)S(1)}, u32[]{:S(2)}, u32[]{:S(2)}) collective-permute-start(f32[256,512]{1,0:T(8,128)S(1)} %fusion.55), channel_id=1, source_target_pairs={{4,6},{6,4},{5,7},{7,5},{8,10},{10,8},{9,11},{11,9},{20,22},{22,20... | collective-permute-start | bytes 1572872 | tf_op jit(solution)/shard_map/cv0/ppermute | solution.py:66
  88.3 20.5 %collective-permute-start.19 = (bf16[512,512]{1,0:T(8,128)(2,1)}, bf16[512,512]{1,0:T(8,128)(2,1)S(1)}, u32[]{:S(2)}, u32[]{:S(2)}) collective-permute-start(bf16[512,512]{1,0:T(8,128)(2,1)} %pad_maximum_fusion.28), channel_id=1, source_target_pairs={{0,8},{2,10},{12,4},{14,6},{1,9},{3,11},{13,5},{15,7},{16,24},{18,... | collective-permute-start | bytes 1572872 | tf_op jit(solution)/shard_map/over2/ppermute | solution.py:59
  92.2 25.3 %collective-permute-start.9 = (f32[512,512]{1,0:T(8,128)}, f32[512,512]{1,0:T(8,128)}, u32[]{:S(2)}, u32[]{:S(2)}) collective-permute-start(f32[512,512]{1,0:T(8,128)} %fusion.37), channel_id=1, source_target_pairs={{4,6},{6,4},{5,7},{7,5},{8,10},{10,8},{9,11},{11,9},{20,22},{22,20... | collective-permute-start | bytes 3145736 | tf_op jit(solution)/shard_map/c1/ppermute | solution.py:66
  103.8 1.0 slice-start
  107.3 25.4 %collective-permute-start.14 = (f32[512,1024]{1,0:T(8,128)S(1)}, f32[512,1024]{1,0:T(8,128)S(1)}, u32[]{:S(2)}, u32[]{:S(2)}) collective-permute-start(f32[512,1024]{1,0:T(8,128)S(1)} %fusion.34), channel_id=1, source_target_pairs={{1,3},{3,1},{13,15},{15,13},{17,19},{19,17},{29,31},{31,29}} | collective-permute-start | bytes 6291464 | tf_op jit(solution)/shard_map/e0/ppermute | solution.py:66
  108.2 10.1 %collective-permute-start.18 = (bf16[512,512]{1,0:T(8,128)(2,1)S(1)}, bf16[512,512]{1,0:T(8,128)(2,1)S(1)}, u32[]{:S(2)}, u32[]{:S(2)}) collective-permute-start(bf16[512,512]{1,0:T(8,128)(2,1)S(1)} %get-tuple-element.44), channel_id=1, source_target_pairs={{4,8},{6,10},{8,4},{10,6},{5,9},{7,11},{9,5},{11,7},{20,24},{22,26... | collective-permute-start | bytes 1572872 | tf_op jit(solution)/shard_map/middle3/ppermute | solution.py:59
  110.2 14.8 %collective-permute-start.20 = (bf16[512,512]{1,0:T(8,128)(2,1)S(1)}, bf16[512,512]{1,0:T(8,128)(2,1)S(1)}, u32[]{:S(2)}, u32[]{:S(2)}) collective-permute-start(bf16[512,512]{1,0:T(8,128)(2,1)S(1)} %get-tuple-element.44), channel_id=1, source_target_pairs={{0,8},{2,10},{12,4},{14,6},{1,9},{3,11},{13,5},{15,7},{16,24},{18,... | collective-permute-start | bytes 1572872 | tf_op jit(solution)/shard_map/over3/ppermute | solution.py:59
  116.1 10.4 %collective-permute-start.24 = (bf16[1024,512]{1,0:T(8,128)(2,1)S(1)}, bf16[1024,512]{1,0:T(8,128)(2,1)S(1)}, u32[]{:S(2)}, u32[]{:S(2)}) collective-permute-start(bf16[1024,512]{1,0:T(8,128)(2,1)S(1)} %pad_maximum_fusion.12), channel_id=1, source_target_pairs={{5,1},{7,3},{9,13},{11,15},{21,17},{23,19},{25,29},{27,31}} | collective-permute-start | bytes 3145736 | tf_op jit(solution)/shard_map/forward2/ppermute | solution.py:59
  117.6 10.9 %collective-permute-start.21 = (f32[512,512]{1,0:T(8,128)S(1)}, f32[512,512]{1,0:T(8,128)S(1)}, u32[]{:S(2)}, u32[]{:S(2)}) collective-permute-start(f32[512,512]{1,0:T(8,128)S(1)} %fusion.36), channel_id=1, source_target_pairs={{4,6},{6,4},{5,7},{7,5},{8,10},{10,8},{9,11},{11,9},{20,22},{22,20... | collective-permute-start | bytes 3145736 | tf_op jit(solution)/shard_map/c2/ppermute | solution.py:66
  125.0 6.8 %collective-permute-start.31 = (f32[512,512]{1,0:T(8,128)S(1)}, f32[512,512]{1,0:T(8,128)S(1)}, u32[]{:S(2)}, u32[]{:S(2)}) collective-permute-start(f32[512,512]{1,0:T(8,128)S(1)} %pad_maximum_fusion.14), channel_id=1, source_target_pairs={{0,1},{1,0},{2,3},{3,2},{4,5},{5,4},{6,7},{7,6},{8,9},{9,8},{10,11... | collective-permute-start | bytes 3145736 | tf_op jit(solution)/shard_map/scores/ppermute | solution.py:70
  126.4 13.8 %collective-permute-start.25 = (bf16[1024,512]{1,0:T(8,128)(2,1)S(1)}, bf16[1024,512]{1,0:T(8,128)(2,1)S(1)}, u32[]{:S(2)}, u32[]{:S(2)}) collective-permute-start(bf16[1024,512]{1,0:T(8,128)(2,1)S(1)} %pad_maximum_fusion.11), channel_id=1, source_target_pairs={{5,1},{7,3},{9,13},{11,15},{21,17},{23,19},{25,29},{27,31}} | collective-permute-start | bytes 3145736 | tf_op jit(solution)/shard_map/forward3/ppermute | solution.py:59
  128.5 15.2 %collective-permute-start.22 = (f32[512,512]{1,0:T(8,128)S(1)}, f32[512,512]{1,0:T(8,128)S(1)}, u32[]{:S(2)}, u32[]{:S(2)}) collective-permute-start(f32[512,512]{1,0:T(8,128)S(1)} %fusion.35), channel_id=1, source_target_pairs={{4,6},{6,4},{5,7},{7,5},{8,10},{10,8},{9,11},{11,9},{20,22},{22,20... | collective-permute-start | bytes 3145736 | tf_op jit(solution)/shard_map/c3/ppermute | solution.py:66
  130.5 28.6 %collective-permute-start.28 = (f32[256,512]{1,0:T(8,128)S(1)}, f32[256,512]{1,0:T(8,128)S(1)}, u32[]{:S(2)}, u32[]{:S(2)}) collective-permute-start(f32[256,512]{1,0:T(8,128)S(1)} %slice.118), channel_id=1, source_target_pairs={{4,0},{6,2},{8,12},{10,14},{20,16},{22,18},{24,28},{26,30}} | collective-permute-start | bytes 1572872 | tf_op jit(solution)/shard_map/end_diag/ppermute | solution.py:59
  132.8 8.8 %collective-permute-start.26 = (f32[512,512]{1,0:T(8,128)S(1)}, f32[512,512]{1,0:T(8,128)S(1)}, u32[]{:S(2)}, u32[]{:S(2)}) collective-permute-start(f32[512,512]{1,0:T(8,128)S(1)} %fusion.32), channel_id=1, source_target_pairs={{1,3},{3,1},{13,15},{15,13},{17,19},{19,17},{29,31},{31,29}} | collective-permute-start | bytes 3145736 | tf_op jit(solution)/shard_map/e2/ppermute | solution.py:66
  133.7 2.4 %copy-start.6 = (f32[256,512]{1,0:T(8,128)S(1)}, f32[256,512]{1,0:T(8,128)}, u32[]{:S(2)}) copy-start(f32[256,512]{1,0:T(8,128)} %fusion.15) | copy-start | bytes 1572868
  138.9 40.4 %collective-permute-start.10 = (f32[256,1024]{1,0:T(8,128)S(1)}, f32[256,1024]{1,0:T(8,128)S(1)}, u32[]{:S(2)}, u32[]{:S(2)}) collective-permute-start(f32[256,1024]{1,0:T(8,128)S(1)} %pad_maximum_fusion.8), channel_id=1, source_target_pairs={{4,0},{6,2},{8,12},{10,14},{20,16},{22,18},{24,28},{26,30}} | collective-permute-start | bytes 3145736 | tf_op jit(solution)/shard_map/end_diag/ppermute | solution.py:59
  141.6 6.0 %collective-permute-start.27 = (f32[512,512]{1,0:T(8,128)S(1)}, f32[512,512]{1,0:T(8,128)S(1)}, u32[]{:S(2)}, u32[]{:S(2)}) collective-permute-start(f32[512,512]{1,0:T(8,128)S(1)} %fusion.33), channel_id=1, source_target_pairs={{1,3},{3,1},{13,15},{15,13},{17,19},{19,17},{29,31},{31,29}} | collective-permute-start | bytes 3145736 | tf_op jit(solution)/shard_map/e3/ppermute | solution.py:66
  142.3 38.9 %collective-permute-start.29 = (f32[128,1024]{1,0:T(8,128)S(1)}, f32[128,1024]{1,0:T(8,128)S(1)}, u32[]{:S(2)}, u32[]{:S(2)}) collective-permute-start(f32[128,1024]{1,0:T(8,128)S(1)} %pad_maximum_fusion.31), channel_id=1, source_target_pairs={{1,0},{3,2},{5,4},{7,6},{9,8},{11,10},{13,12},{15,14},{17,16},{19,... | collective-permute-start | bytes 1572872 | tf_op jit(solution)/shard_map/low_cross/ppermute | solution.py:249
  145.0 34.3 %collective-permute-start.23 = (f32[256,512]{1,0:T(8,128)S(1)}, f32[256,512]{1,0:T(8,128)S(1)}, u32[]{:S(2)}, u32[]{:S(2)}) collective-permute-start(f32[256,512]{1,0:T(8,128)S(1)} %slice.113), channel_id=1, source_target_pairs={{4,0},{6,2},{8,12},{10,14},{20,16},{22,18},{24,28},{26,30}} | collective-permute-start | bytes 1572872 | tf_op jit(solution)/shard_map/end_diag/ppermute | solution.py:59
  149.0 32.3 %collective-permute-start.30 = (f32[128,1024]{1,0:T(8,128)S(1)}, f32[128,1024]{1,0:T(8,128)S(1)}, u32[]{:S(2)}, u32[]{:S(2)}) collective-permute-start(f32[128,1024]{1,0:T(8,128)S(1)} %pad_maximum_fusion.32), channel_id=1, source_target_pairs={{1,0},{3,2},{5,4},{7,6},{9,8},{11,10},{13,12},{15,14},{17,16},{19,... | collective-permute-start | bytes 1572872 | tf_op jit(solution)/shard_map/low_cross/ppermute | solution.py:249
